TPU v7x, 128 devices: a whole 4x4x4 slice. The times are simulated.
128 devices in a mesh: rank: 4 (over z), tiles: 32 (over x, y, core).
Axes of the slice: x: 4, y: 4, z: 4, core: 2. Of those that a mesh axis runs over, the one named last changes fastest.
Arguments:
- user_factor: bfloat16 [32768, 1024], P('tiles', 'rank'), may hold values from -1 to 1
- item_factor: bfloat16 [8192, 1024], P('tiles', 'rank'), may hold values from -1 to 1
- context_factor: bfloat16 [256, 1024], P(None, 'rank'), may hold values from -5 to 5
- tile_user: int32 [4096], P('tiles'), may hold values from 0 to 7
- tile_item: int32 [4096], P('tiles'), may hold values from 0 to 63
- tile_context: int32 [4096], P('tiles'), may hold values from 0 to 255
- tile_count: int32 [32], P('tiles'), may hold values from 32 to 128, as said below
- tile_mask: int32 [4096, 128, 128], P('tiles'), may hold values 0 or 1
- item_slot: int32 [64], replicated, may hold values from 0 to 63, each once
Outputs:
- user_grad: float32 [32768, 1024], P('tiles', 'rank')
- item_grad: float32 [8192, 1024], P('tiles', 'rank')
- context_grad: float32 [256, 1024], P(None, 'rank')
Inputs may be any that keep to these rules, and one draw needn't show every extreme that they name: `tile_count`: some index of tiles uses all 128 slots in every draw.
All inputs are finite; a program needn't handle non-finite values. No bound on the sum of `tile_mask` on one device may be relied on, other than what follows from the above.
Results may differ from a plain program's by a relative error of at most 0.0031.
Values may be sent and summed in bfloat16 or wider, within the bound.
A program may use at most 128 MiB of HBM per device.

v0:
```python
import jax
import jax.numpy as jnp
from jax import lax
from jax.sharding import PartitionSpec as P


def weigh(prediction, maskf, live):
    return (live * (1.0 + 4.0 * maskf) * (prediction - maskf) / 128.0).astype(jnp.bfloat16)


def local(
    user_factor,
    item_factor,
    context_factor,
    tile_user,
    tile_item,
    tile_context,
    tile_count,
    tile_mask,
    item_slot,
):
    slots_dev = tile_user.shape[0]
    side = tile_mask.shape[1]
    width = user_factor.shape[1]
    ublocks = user_factor.reshape(-1, side, width)
    gathered = lax.all_gather(item_factor, "tiles", axis=0, tiled=True).reshape(-1, side, width)
    nblocks = gathered.shape[0]
    hot_id = (tile_item[:, None] == jnp.arange(nblocks)[None, :]).astype(jnp.int32)
    slots = jnp.sum(hot_id * item_slot[None, :], axis=1)
    users = ublocks[tile_user]
    items = gathered[slots]
    nctx = context_factor.shape[0]
    chot = tile_context[:, None] == jnp.arange(nctx)[None, :]
    crow = jnp.dot(chot.astype(jnp.bfloat16), context_factor, preferred_element_type=jnp.float32)
    item_context = (items * crow[:, None, :]).astype(jnp.bfloat16)
    user_context = (users * crow[:, None, :]).astype(jnp.bfloat16)
    partial_value = jnp.einsum(
        "tur,tir->tui", users, item_context, preferred_element_type=jnp.float32
    )
    live = (jnp.arange(slots_dev) < tile_count[0]).astype(jnp.float32)[:, None, None]
    maskf = tile_mask.astype(jnp.float32)
    prediction = lax.psum(partial_value, "rank")
    resid = weigh(prediction, maskf, live)
    pulled = jnp.einsum("tui,tir->tur", resid, items, preferred_element_type=jnp.float32)
    user_grad = (
        jnp.zeros((ublocks.shape[0], side, width), jnp.float32)
        .at[tile_user]
        .add(pulled * crow[:, None, :])
    )
    iterm = jnp.einsum("tui,tur->tir", resid, user_context, preferred_element_type=jnp.float32)
    dense = jnp.zeros((nblocks, side, width), jnp.float32).at[slots].add(iterm)
    item_grad = lax.psum_scatter(dense, "tiles", scatter_dimension=0, tiled=True)
    cterm = jnp.sum(users * pulled, axis=1)
    ctx_part = jnp.dot(chot.astype(jnp.float32).T, cterm, precision=lax.Precision.HIGHEST)
    context_grad = lax.psum(ctx_part, "tiles")
    return (user_grad.reshape(-1, width), item_grad.reshape(-1, width), context_grad)


def solution(mesh):
    return jax.shard_map(
        local,
        mesh=mesh,
        in_specs=(
            P("tiles", "rank"),
            P("tiles", "rank"),
            P(None, "rank"),
            P("tiles"),
            P("tiles"),
            P("tiles"),
            P("tiles"),
            P("tiles", None, None),
            P(),
        ),
        out_specs=(P("tiles", "rank"), P("tiles", "rank"), P(None, "rank")),
        check_vma=False,
    )
```

profile of v0, /device:TPU:0, one launch (start us, length us, event | category | flops | bytes accessed | tf_op | source)
XLA Modules:
  0.0 467.1 jit_solution(16109951908005422381)
XLA Ops:
  7.2 0.0 copy-start
  7.2 0.0 all-gather.2.cloned.1.call-start
  7.2 0.7 all-gather.2.cloned.1.call-update
  7.9 0.0 all-reduce.3.cloned.1.call-start
  8.0 0.7 compare_select_fusion.1
  8.6 0.0 copy-done
  8.6 0.0 copy-start.6
  8.6 0.0 copy-start.7
  8.7 0.0 copy-start.4
  8.7 0.0 copy-start.5
  8.7 6.5 %gather_fusion = bf16[128,128,256]{2,1,0:T(8,128)(2,1)} fusion(bf16[8,128,256]{2,1,0:T(8,128)(2,1)S(1)} %bitcast.16, s32[1024]{0:T(1024)S(1)} %pad_clamp_fusion.1), kind=kCustom, calls=%fused_computation | custom fusion | bytes 16777728 | tf_op jit(solution)/shard_map/gather | solution.py:30
  15.2 0.0 copy-done.6
  15.2 0.0 copy-done.7
  15.2 0.1 select_reduce_fusion
  15.3 0.0 copy-done.4
  15.3 0.0 copy-done.5
  15.3 0.2 fusion.8
  15.6 43.2 %all-gather.2.cloned.1.call-done = bf16[8192,256]{1,0:T(8,128)(2,1)} async-done(((bf16[256,256]{1,0:T(8,128)(2,1)}), bf16[8192,256]{1,0:T(8,128)(2,1)}) %all-gather.2.cloned.1.call-update) | async-done | bytes 4194320 | tf_op jit(solution)/shard_map/all_gather | solution.py:26
  58.7 8.8 %gather_fusion.1 = bf16[128,128,256]{2,1,0:T(8,128)(2,1)} fusion(bf16[64,128,256]{2,1,0:T(8,128)(2,1)} %bitcast.18, s32[1024]{0:T(1024)S(1)} %pad_clamp_fusion), kind=kCustom, calls=%fused_computation.1 | custom fusion | bytes 16777728 | tf_op jit(solution)/shard_map/gather | solution.py:31
  67.5 11.3 %fusion.2 = f32[128,128,128]{2,1,0:T(8,128)} fusion(bf16[128,128,256]{2,1,0:T(8,128)(2,1)} %gather_fusion, bf16[128,128,256]{2,1,0:T(8,128)(2,1)} %gather_fusion.1, f32[128,256]{1,0:T(8,128)S(1)} %fusion.8), kind=kOutput, calls=%fused_computation.9 | convolution fusion | flops 1086324736 | bytes 25296896 | tf_op jit(solution)/shard_map/tur,tir->tui/dot_general | solution.py:37
  78.8 0.0 all-reduce.3.cloned.1.call-update
  78.8 0.0 all-reduce.5.cloned.1.call-start
  79.5 159.3 %all-reduce.3.cloned.1.call-done = f32[128,128,128]{2,1,0:T(8,128)} async-done(((f32[128,128,128]{2,1,0:T(8,128)}), f32[128,128,128]{2,1,0:T(8,128)}) %all-reduce.3.cloned.1.call-update) | async-done | bytes 8388624 | tf_op jit(solution)/shard_map/psum | solution.py:42
  238.9 7.2 %multiply_convert_fusion.2 = bf16[128,128,128]{2,1,0:T(8,128)(2,1)S(1)} fusion(f32[128,128,128]{2,1,0:T(8,128)} %all-reduce.3.cloned.1.call-done, s32[128,128,128]{2,1,0:T(8,128)} %param.16, f32[128]{0:T(128)S(1)} %compare_convert_fusion), kind=kLoop, calls=%fused_computation.11 | loop fusion | flops 16777216 | bytes 20972032 | tf_op jit(solution)/shard_map/convert_element_type | solution.py:8
  246.0 0.0 copy-start.3
  246.1 13.8 %fusion.1 = (f32[128,256]{1,0:T(8,128)S(1)}, f32[128,128,256]{2,1,0:T(8,128)}) fusion(bf16[128,128,256]{2,1,0:T(8,128)(2,1)} %gather_fusion, f32[128,256]{1,0:T(8,128)S(1)} %fusion.8, bf16[128,128,128]{2,1,0:T(8,128)(2,1)S(1)} %multiply_convert_fusion.2, bf16[128,128,256]{2,1,0:T(8,128)(2,1)} %gather_fusion.1), kind=kOutput, calls=%fused_computation.7 | convolution fusion | flops 1090486272 | bytes 38010880 | tf_op jit(solution)/shard_map/tui,tir->tur/dot_general | solution.py:44
  259.9 0.0 copy-done.3
  259.9 1.1 fusion.7
  261.0 0.0 all-reduce.5.cloned.1.call-update
  261.0 0.2 reduce-scatter.2.cloned.1.call-start
  261.2 12.8 %fusion.3 = f32[128,128,256]{2,1,0:T(8,128)} fusion(bf16[128,128,128]{2,1,0:T(8,128)(2,1)} %copy-done.3, bf16[128,128,256]{2,1,0:T(8,128)(2,1)} %gather_fusion, f32[128,256]{1,0:T(8,128)S(1)} %fusion.8), kind=kOutput, calls=%fused_computation.10 | convolution fusion | flops 1086324736 | bytes 29491200 | tf_op jit(solution)/shard_map/tui,tur->tir/dot_general | solution.py:50
  274.0 4.2 broadcast_in_dim.8
  278.3 38.5 %scatter_fusion.1 = f32[64,128,256]{2,1,0:T(8,128)} fusion(f32[64,128,256]{2,1,0:T(8,128)} %broadcast_in_dim.8, s32[128]{0:T(128)S(1)} %fusion.11, f32[128,128,256]{2,1,0:T(8,128)} %fusion.3), kind=kCustom, calls=%fused_computation.3 | custom fusion | flops 4194304 | bytes 50332160 | tf_op jit(solution)/shard_map/scatter-add | solution.py:51
  316.8 0.0 reduce-scatter.2.cloned.1.call-update
  316.9 0.1 broadcast_in_dim.6
  316.9 0.0 copy-start.1
  317.0 24.2 %scatter_fusion = f32[8,128,256]{2,1,0:T(8,128)S(1)} fusion(f32[8,128,256]{2,1,0:T(8,128)S(1)} %broadcast_in_dim.6, s32[128]{0:T(128)S(1)} %compare_select_fusion.1, f32[128,128,256]{2,1,0:T(8,128)} %get-tuple-element.4), kind=kCustom, calls=%fused_computation.2 | custom fusion | flops 4194304 | bytes 50332160 | tf_op jit(solution)/shard_map/scatter-add | solution.py:48
  341.2 0.0 copy-start.2
  341.2 20.9 %all-reduce.5.cloned.1.call-done = f32[256,256]{1,0:T(8,128)} async-done(((f32[256,256]{1,0:T(8,128)}), f32[256,256]{1,0:T(8,128)}) %all-reduce.5.cloned.1.call-update) | async-done | bytes 262160 | tf_op jit(solution)/shard_map/psum | solution.py:55
  362.1 96.9 %reduce-scatter.2.cloned.1.call-done = f32[2,128,256]{2,1,0:T(8,128)} async-done(((f32[64,128,256]{2,1,0:T(8,128)}), f32[2,128,256]{2,1,0:T(8,128)}) %reduce-scatter.2.cloned.1.call-update) | async-done | bytes 262160 | tf_op jit(solution)/shard_map/reduce_scatter | solution.py:52
  458.9 1.7 copy.20
  460.6 0.0 copy-done.2
  460.6 0.0 copy-done.1
  (4 shorter events, 0.0 us)
Async XLA Ops:
  7.2 1.5 copy-start
  7.2 51.5 %all-gather.2.cloned.1.call-start = ((), (), s32[]{:S(2)}) async-start(), calls=%async_computation.1 | async-start | bytes 4325376 | tf_op jit(solution)/shard_map/all_gather | solution.py:26
  7.9 231.0 %all-reduce.3.cloned.1.call-start = ((), (), s32[]{:S(2)}) async-start(), calls=%async_computation.2 | async-start | bytes 16777216 | tf_op jit(solution)/shard_map/psum | solution.py:42
  8.6 6.6 %copy-start.6 = (s32[64]{0:T(128)S(1)}, s32[64]{0:T(128)}, u32[]{:S(2)}) copy-start(s32[64]{0:T(128)} %param.17) | copy-start | bytes 772
  8.6 6.6 %copy-start.7 = (s32[128]{0:T(128)S(1)}, s32[128]{0:T(128)}, u32[]{:S(2)}) copy-start(s32[128]{0:T(128)} %param.13) | copy-start | bytes 1540
  8.7 6.7 %copy-start.4 = (bf16[256,256]{1,0:T(8,128)(2,1)S(1)}, bf16[256,256]{1,0:T(8,128)(2,1)}, u32[]{:S(2)}) copy-start(bf16[256,256]{1,0:T(8,128)(2,1)} %param.11) | copy-start | bytes 393220
  8.7 6.7 %copy-start.5 = (s32[128]{0:T(128)S(1)}, s32[128]{0:T(128)}, u32[]{:S(2)}) copy-start(s32[128]{0:T(128)} %param.14) | copy-start | bytes 1540
  78.8 283.2 %all-reduce.5.cloned.1.call-start = ((), (), s32[]{:S(2)}) async-start(), calls=%async_computation.4 | async-start | bytes 524288 | tf_op jit(solution)/shard_map/psum | solution.py:55
  246.0 13.9 %copy-start.3 = (bf16[128,128,128]{2,1,0:T(8,128)(2,1)}, bf16[128,128,128]{2,1,0:T(8,128)(2,1)S(1)}, u32[]{:S(2)}) copy-start(bf16[128,128,128]{2,1,0:T(8,128)(2,1)S(1)} %multiply_convert_fusion.2) | copy-start | bytes 12582916
  261.0 197.9 %reduce-scatter.2.cloned.1.call-start = ((), (), s32[]{:S(2)}) async-start(), calls=%async_computation.3 | async-start | bytes 8650752 | tf_op jit(solution)/shard_map/reduce_scatter | solution.py:52
  316.9 143.7 %copy-start.1 = (bf16[1024,256]{1,0:T(8,128)(2,1)S(1)}, bf16[1024,256]{1,0:T(8,128)(2,1)}, u32[]{:S(2)}) copy-start(bf16[1024,256]{1,0:T(8,128)(2,1)} %param.9) | copy-start | bytes 1572868
  341.2 119.4 %copy-start.2 = (f32[8,128,256]{2,1,0:T(8,128)}, f32[8,128,256]{2,1,0:T(8,128)S(1)}, u32[]{:S(2)}) copy-start(f32[8,128,256]{2,1,0:T(8,128)S(1)} %scatter_fusion) | copy-start | bytes 3145732
Sparse Core Ops, SparseCore 0:
  10.3 48.3 all-gather.1
  79.0 159.8 all-reduce.2
  261.1 100.8 all-reduce.4
  366.7 92.2 reduce-scatter.1
where the time goes:
time: 468 us; the launch traced here: 467 us
  waiting for transfers between devices  321 us (69%)
  other arithmetic  70.7 us (15%)
  matrix products  39.3 us (8%)
  local copies, waits for them, and re-layouts  21.3 us (5%)
  between operations  14.5 us (3%)
    psum x1, waiting for transfers between devices, local(): prediction = lax.psum(partial_value, 'rank')  159 us
    reduce_scatter x1, waiting for transfers between devices, local(): lax.psum_scatter(dense, 'tiles', scatter_dimension=0, tiled=True)  96.9 us
    all_gather x1, waiting for transfers between devices, local(): lax.all_gather(item_factor, 'tiles', axis=0, tiled=True)  43.2 us
    scatter-add x1, other arithmetic, local(): dense = jnp.zeros((nblocks, side, width), jnp.float32).at[slots].add(iterm)  38.5 us
    scatter-add x1, other arithmetic, local(): user_grad = jnp.zeros((ublocks.shape[0], side, width), jnp.float32).at[ti...  24.2 us
    psum x1, waiting for transfers between devices, local(): context_grad = lax.psum(ctx_part, 'tiles')  20.9 us
    dot_general x1, matrix products, local(): jnp.einsum('tui,tir->tur', resid, items, preferred_element_type=jnp.float32)  13.8 us
    dot_general x1, matrix products, local(): jnp.einsum('tui,tur->tir', resid, user_context, preferred_element_type=jn...  12.8 us
  transfers between devices with their start and end apart: 4, of which 4 were waited for; matrix products, arithmetic and copies ran while one was open for 19% of the time, Pallas kernels for 0%

commit v1 on v0

v1 whole, which is shorter than its diff:
```python
import functools

import jax
import jax.numpy as jnp
from jax import lax
from jax.experimental import pallas as pl
from jax.experimental.pallas import tpu as pltpu
from jax.sharding import PartitionSpec as P

MESH = pl.DeviceIdType.MESH
BF16 = jnp.bfloat16
F32 = jnp.float32
NB = 8
PER = 4
SIDE = 128
WIDTH = 256


def kernel(
    place_ref,
    user_ref,
    perm_ref,
    live_ref,
    keep_ref,
    last_ref,
    has_ref,
    users_ref,
    shard_ref,
    crow_ref,
    mask_hbm,
    ugrad_ref,
    ipart_ref,
    cterm_ref,
    items,
    mask,
    part,
    send1,
    recv1,
    send2,
    recv2,
    resid,
    run,
    segs,
    ahot,
    icb,
    mask_sem,
    ag_send,
    ag_recv,
    z_send,
    z_recv,
):
    z = lax.axis_index("rank")
    t = lax.axis_index("tiles")
    c = lax.rem(t, 2)
    y = lax.rem(t // 2, 4)
    x = t // 8
    f = x * (1 - c) + y * c
    s = y * (1 - c) + x * c

    def dev(fi, si):
        fi, si = lax.rem(fi + 4, 4), lax.rem(si + 4, 4)
        xi = fi * (1 - c) + si * c
        yi = si * (1 - c) + fi * c
        return {"rank": z, "tiles": (xi * 4 + yi) * 2 + c}

    def devz(d):
        return {"rank": lax.rem(z + d + 4, 4), "tiles": t}

    sib = {"rank": z, "tiles": t + 1 - 2 * c}
    partners = (dev(f + 1, s), dev(f - 1, s), dev(f, s + 1), dev(f, s - 1), devz(1), devz(-1), sib)
    mask_copy = pltpu.make_async_copy(mask_hbm, mask, mask_sem)
    mask_copy.start()
    barrier = pltpu.get_barrier_semaphore()
    for p in partners:
        pl.semaphore_signal(barrier, inc=1, device_id=p, device_id_type=MESH)
    pl.semaphore_wait(barrier, len(partners))

    def rcopy(src, dst, ss, rs, to):
        return pltpu.make_async_remote_copy(
            src_ref=src, dst_ref=dst, send_sem=ss, recv_sem=rs, device_id=to, device_id_type=MESH
        )

    started = []

    def ag(k, start, size, to, src=None):
        view = items.at[pl.ds(start, size)]
        cp = rcopy(view if src is None else src, view, ag_send.at[k], ag_recv.at[k], to)
        cp.start()
        started.append(cp)

    def got(k, start, size):
        view = items.at[pl.ds(start, size)]
        rcopy(view, view, ag_send.at[k], ag_recv.at[k], sib).wait_recv()

    def blk(ci, si, fi):
        return ((ci * 4 + lax.rem(si + 4, 4)) * 4 + lax.rem(fi + 4, 4)) * 2

    ag(0, blk(c, s, f), 2, dev(f + 1, s), shard_ref)
    ag(1, blk(c, s, f), 2, dev(f - 1, s), shard_ref)
    items[pl.ds(blk(c, s, f), 2)] = shard_ref[...]
    got(0, blk(c, s, f - 1), 2)
    ag(2, blk(c, s, f - 1), 1, dev(f + 1, s))
    got(1, blk(c, s, f + 1), 2)
    ag(3, blk(c, s, f + 1) + 1, 1, dev(f - 1, s))
    got(2, blk(c, s, f + 2), 1)
    got(3, blk(c, s, f + 2) + 1, 1)
    slab = lambda si: blk(c, si, f * 0)
    other = lambda si: blk(1 - c, si, f * 0)
    ag(4, slab(s), 8, dev(f, s + 1))
    ag(5, slab(s), 8, dev(f, s - 1))
    ag(6, slab(s), 8, sib)
    got(4, slab(s - 1), 8)
    ag(7, slab(s - 1), 4, dev(f, s + 1))
    ag(8, slab(s - 1), 8, sib)
    got(5, slab(s + 1), 8)
    ag(9, slab(s + 1) + 4, 4, dev(f, s - 1))
    ag(10, slab(s + 1), 8, sib)
    got(7, slab(s + 2), 4)
    got(9, slab(s + 2) + 4, 4)
    ag(11, slab(s + 2), 8, sib)
    got(6, other(f), 8)
    got(8, other(f - 1), 8)
    got(10, other(f + 1), 8)
    got(11, other(f + 2), 8)
    mask_copy.wait()
    ugrad_ref[...] = jnp.zeros_like(ugrad_ref)
    run[...] = jnp.zeros_like(run)

    right, left = devz(1), devz(-1)

    def zcopies(ph, j):
        o = z
        if ph == 0:
            return (
                rcopy(send1.at[j, pl.ds(0, 2)], recv1.at[j, 0], z_send.at[ph, j, 0], z_recv.at[ph, j, 0], right),
                rcopy(send1.at[j, pl.ds(2, 2)], recv1.at[j, 1], z_send.at[ph, j, 1], z_recv.at[ph, j, 1], left),
            )
        if ph == 1:
            return (
                rcopy(send2.at[j, 0], recv2.at[j, 0], z_send.at[ph, j, 0], z_recv.at[ph, j, 0], right),
                rcopy(send2.at[j, 1], recv2.at[j, 1], z_send.at[ph, j, 1], z_recv.at[ph, j, 1], left),
            )
        if ph == 2:
            return (
                rcopy(resid.at[j, o], resid.at[j, o], z_send.at[ph, j, 0], z_recv.at[ph, j, 0], right),
                rcopy(resid.at[j, o], resid.at[j, o], z_send.at[ph, j, 1], z_recv.at[ph, j, 1], left),
            )
        lo, hi = lax.rem(z + 3, 4), lax.rem(z + 1, 4)
        a = resid.at[j, lo, pl.ds(0, 2)]
        b = resid.at[j, hi, pl.ds(2, 2)]
        return (
            rcopy(a, a, z_send.at[ph, j, 0], z_recv.at[ph, j, 0], right),
            rcopy(b, b, z_send.at[ph, j, 1], z_recv.at[ph, j, 1], left),
        )

    def zwait(ph, j):
        lo, hi, far = lax.rem(z + 3, 4), lax.rem(z + 1, 4), lax.rem(z + 2, 4)
        if ph == 0:
            views = (recv1.at[j, 0], recv1.at[j, 1])
        elif ph == 1:
            views = (recv2.at[j, 0], recv2.at[j, 1])
        elif ph == 2:
            views = (resid.at[j, lo], resid.at[j, hi])
        else:
            views = (resid.at[j, far, pl.ds(0, 2)], resid.at[j, far, pl.ds(2, 2)])
        for d in range(2):
            rcopy(views[d], views[d], z_send.at[ph, j, d], z_recv.at[ph, j, d], right).wait_recv()

    def item_context(p):
        it = items[place_ref[p]].astype(F32)
        return (it * crow_ref[pl.ds(p, 1), :]).astype(BF16)

    def predict(j):
        slot = lax.rem(j, 4)

        def tile(n, _):
            o, k = n // PER, lax.rem(n, PER)
            p = j * 16 + n
            pr = lax.dot_general(
                users_ref[user_ref[p]], item_context(p), (((1,), (1,)), ((), ())), preferred_element_type=F32
            )
            part[slot, o, k] = pr
            return 0

        lax.fori_loop(0, 16, tile, 0)
        send1[j] = part[slot, lax.rem(z + 2, 4)].astype(BF16)
        for cp in zcopies(0, j):
            cp.start()

    def combine(j):
        slot = lax.rem(j, 4)
        hi, lo = lax.rem(z + 1, 4), lax.rem(z + 3, 4)
        zwait(0, j)
        send2[j, 0, pl.ds(0, 2)] = (part[slot, hi, pl.ds(0, 2)] + recv1[j, 0].astype(F32)).astype(BF16)
        send2[j, 0, pl.ds(2, 2)] = part[slot, hi, pl.ds(2, 2)].astype(BF16)
        send2[j, 1, pl.ds(0, 2)] = part[slot, lo, pl.ds(0, 2)].astype(BF16)
        send2[j, 1, pl.ds(2, 2)] = (part[slot, lo, pl.ds(2, 2)] + recv1[j, 1].astype(F32)).astype(BF16)
        for cp in zcopies(1, j):
            cp.start()

    def weigh(j):
        slot = lax.rem(j, 4)
        zwait(1, j)
        for k in range(PER):
            p = j * 16 + z * PER + k
            pr = part[slot, z, k] + recv2[j, 0, k].astype(F32) + recv2[j, 1, k].astype(F32)
            m = mask[perm_ref[p]].astype(F32)
            resid[j, z, k] = (live_ref[p] * (1.0 + 4.0 * m) * (pr - m) * (1.0 / 128.0)).astype(BF16)
        for cp in zcopies(2, j):
            cp.start()

    def forward(j):
        zwait(2, j)
        for cp in zcopies(3, j):
            cp.start()

    def gradients(j):
        zwait(3, j)

        def group(o, _):
            for k in range(PER):
                p = j * 16 + o * PER + k
                r = resid[j, o, k]
                u = user_ref[p]
                for b in range(8):
                    ahot[pl.ds(b * SIDE, SIDE), pl.ds(k * SIDE, SIDE)] = jnp.where(u == b, r, jnp.zeros_like(r))
                it = items[place_ref[p]].astype(F32)
                cr = crow_ref[pl.ds(p, 1), :]
                icb[pl.ds(k * SIDE, SIDE), :] = (it * cr).astype(BF16)
                q = lax.dot_general(r, users_ref[u], (((0,), (0,)), ((), ())), preferred_element_type=F32)
                cterm_ref[pl.ds(p, 1), :] = jnp.sum(it * q, axis=0, keepdims=True)
                total = run[...] * keep_ref[p] + q * cr
                run[...] = total
                segs[p] = total.astype(BF16)
            ugrad_ref[...] += jnp.dot(ahot[...], icb[...], preferred_element_type=F32)
            return 0

        lax.fori_loop(0, 4, group, 0)

    def step(i, _):
        @pl.when(i < NB)
        def _():
            predict(i)

        @pl.when((i >= 1) & (i < NB + 1))
        def _():
            combine(i - 1)

        @pl.when((i >= 2) & (i < NB + 2))
        def _():
            weigh(i - 2)

        @pl.when((i >= 3) & (i < NB + 3))
        def _():
            forward(i - 3)

        @pl.when(i >= 4)
        def _():
            gradients(i - 4)

        return 0

    lax.fori_loop(0, NB + 4, step, 0)

    def finish(b, _):
        ipart_ref[b] = segs[last_ref[b]].astype(F32) * has_ref[b]
        return 0

    lax.fori_loop(0, 64, finish, 0)
    for cp in started:
        cp.wait_send()
    for ph in range(4):
        def drain(j, _):
            for cp in zcopies(ph, j):
                cp.wait_send()
            return 0

        lax.fori_loop(0, NB, drain, 0)


def local(
    user_factor,
    item_factor,
    context_factor,
    tile_user,
    tile_item,
    tile_context,
    tile_count,
    tile_mask,
    item_slot,
):
    n = tile_user.shape[0]
    nblocks = item_slot.shape[0]
    nctx = context_factor.shape[0]
    ids = jnp.arange(n, dtype=jnp.int32)
    hot_id = (tile_item[:, None] == jnp.arange(nblocks)[None, :]).astype(jnp.int32)
    slots = jnp.sum(hot_id * item_slot[None, :], axis=1)

    def place_of(block):
        owner, half = block // 2, block % 2
        core, xi, yi = owner % 2, owner // 8, (owner // 2) % 4
        fi = jnp.where(core == 0, xi, yi)
        si = jnp.where(core == 0, yi, xi)
        return ((core * 4 + si) * 4 + fi) * 2 + half

    place = place_of(slots)
    key = place * n + ids
    rank = jnp.sum((key[None, :] < key[:, None]).astype(jnp.int32), axis=1)
    pick = (rank[None, :] == ids[:, None]).astype(jnp.int32)
    live = (ids < tile_count[0]).astype(jnp.int32)
    vals = jnp.stack([place, tile_user, ids, live, tile_context])
    ordered = jnp.sum(pick[None] * vals[:, None, :], axis=2)
    place_s, user_s, perm, live_s, ctx_s = (ordered[i] for i in range(5))
    before = jnp.concatenate([jnp.full((1,), -1, jnp.int32), place_s[:-1]])
    keep = (place_s == before).astype(F32)
    ends = place_of(jnp.arange(nblocks, dtype=jnp.int32))
    last = jnp.maximum(jnp.sum((place[None, :] <= ends[:, None]).astype(jnp.int32), axis=1) - 1, 0)
    has = jnp.any(place[None, :] == ends[:, None], axis=1).astype(F32)
    chot = ctx_s[:, None] == jnp.arange(nctx)[None, :]
    crow = jnp.dot(chot.astype(BF16), context_factor, preferred_element_type=F32)
    smem = pl.BlockSpec(memory_space=pltpu.SMEM)
    vmem = pl.BlockSpec(memory_space=pltpu.VMEM)
    tile2 = (SIDE, SIDE)
    ugrad, ipart, cterm = pl.pallas_call(
        kernel,
        out_shape=(
            jax.ShapeDtypeStruct((1024, WIDTH), F32),
            jax.ShapeDtypeStruct((nblocks, SIDE, WIDTH), F32),
            jax.ShapeDtypeStruct((n, WIDTH), F32),
        ),
        in_specs=[smem] * 7 + [vmem] * 3 + [pl.BlockSpec(memory_space=pl.ANY)],
        out_specs=(vmem,) * 3,
        scratch_shapes=[
            pltpu.VMEM((64, SIDE, WIDTH), BF16),
            pltpu.VMEM((n,) + tile2, jnp.int32),
            pltpu.VMEM((4, 4, PER) + tile2, F32),
            pltpu.VMEM((NB, PER) + tile2, BF16),
            pltpu.VMEM((NB, 2, 2) + tile2, BF16),
            pltpu.VMEM((NB, 2, PER) + tile2, BF16),
            pltpu.VMEM((NB, 2, PER) + tile2, BF16),
            pltpu.VMEM((NB, 4, PER) + tile2, BF16),
            pltpu.VMEM((SIDE, WIDTH), F32),
            pltpu.VMEM((n, SIDE, WIDTH), BF16),
            pltpu.VMEM((1024, PER * SIDE), BF16),
            pltpu.VMEM((PER * SIDE, WIDTH), BF16),
            pltpu.SemaphoreType.DMA,
            pltpu.SemaphoreType.DMA((12,)),
            pltpu.SemaphoreType.DMA((12,)),
            pltpu.SemaphoreType.DMA((4, NB, 2)),
            pltpu.SemaphoreType.DMA((4, NB, 2)),
        ],
        compiler_params=pltpu.CompilerParams(
            collective_id=0, has_side_effects=True, vmem_limit_bytes=62 * 1024 * 1024
        ),
        cost_estimate=pl.CostEstimate(flops=10_000_000_000, bytes_accessed=20_000_000, transcendentals=0),
    )(
        place_s,
        user_s,
        perm,
        live_s.astype(F32),
        keep,
        last,
        has,
        user_factor.reshape(-1, SIDE, WIDTH),
        item_factor.reshape(-1, SIDE, WIDTH),
        crow,
        tile_mask,
    )
    item_grad = lax.psum_scatter(ipart, "tiles", scatter_dimension=0, tiled=True)
    ctx_part = jnp.dot(chot.astype(F32).T, cterm, precision=lax.Precision.HIGHEST)
    context_grad = lax.psum(ctx_part, "tiles")
    return (ugrad, item_grad.reshape(-1, WIDTH), context_grad)


def solution(mesh):
    return jax.shard_map(
        local,
        mesh=mesh,
        in_specs=(
            P("tiles", "rank"),
            P("tiles", "rank"),
            P(None, "rank"),
            P("tiles"),
            P("tiles"),
            P("tiles"),
            P("tiles"),
            P("tiles", None, None),
            P(),
        ),
        out_specs=(P("tiles", "rank"), P("tiles", "rank"), P(None, "rank")),
        check_vma=False,
    )
```

time: 468 us -> 337 us (0.72)
  waiting for transfers between devices: 321 us -> 197 us
  Pallas kernels: 0 us -> 115 us
  other arithmetic: 70.7 us -> 3.86 us
  matrix products: 39.3 us -> 2.94 us
  local copies, waits for them, and re-layouts: 21.3 us -> 3.35 us
    psum x1 -> x0, waiting for transfers between devices: 159 us -> none  [local(): prediction = lax.psum(partial_value, 'rank')]
    pallas_call x0 -> x1, Pallas kernels: none -> 115 us  [local(): pl.pallas_call(kernel, out_shape=(jax.ShapeDtypeStruct((1024, WIDTH), F32...]
    psum x1, waiting for transfers between devices: 20.9 us -> 99.5 us  [local(): context_grad = lax.psum(ctx_part, 'tiles')]
    scatter-add x2 -> x0, other arithmetic: 62.8 us -> none  [the longest x1 38.5 us: local(): dense = jnp.zeros((nblocks, side, width), jnp.float32).at[slots].add(iterm)]
    all_gather x1 -> x0, waiting for transfers between devices: 43.2 us -> none  [local(): lax.all_gather(item_factor, 'tiles', axis=0, tiled=True)]
    dot_general x5 -> x2, matrix products: 39.3 us -> 2.94 us  [the longest x1 2.07 us: local(): jnp.dot(chot.astype(F32).T, cterm, precision=lax.Precision.HIGHEST)]
    gather x2 -> x0, local copies, waits for them, and re-layouts: 15.3 us -> none  [the longest x1 8.75 us: local(): items = gathered[slots]]
    convert_element_type x2 -> x4, other arithmetic: 7.17 us -> 1.2 us  [the longest x1 0.6 us: local(): keep = (place_s == before).astype(F32)]
  transfers between devices with their start and end apart: 4 -> 2, of which waited for: 4 -> 2; matrix products, arithmetic and copies ran while one was open for 19% -> 0% of each run, Pallas kernels for 0% -> 0%
where the time goes in v1:
time: 337 us
  waiting for transfers between devices  197 us (58%)
  Pallas kernels  115 us (34%)
  between operations  14.8 us (4%)
  other arithmetic  3.86 us (1%)
    pallas_call x1, Pallas kernels, local(): pl.pallas_call(kernel, out_shape=(jax.ShapeDtypeStruct((1024, WIDTH), F32...  115 us
    psum x1, waiting for transfers between devices, local(): context_grad = lax.psum(ctx_part, 'tiles')  99.5 us
    reduce_scatter x1, waiting for transfers between devices, local(): lax.psum_scatter(ipart, 'tiles', scatter_dimension=0, tiled=True)  97 us
  transfers between devices with their start and end apart: 2, of which 2 were waited for; matrix products, arithmetic and copies ran while one was open for 0% of the time, Pallas kernels for 0%

profile of v1, /device:TPU:0, one launch (start us, length us, event | category | flops | bytes accessed | tf_op | source)
XLA Modules:
  0.0 337.0 jit_solution(12417984810352336076)
XLA Ops:
  7.2 0.0 copy-start
  7.2 0.0 all-reduce.2.cloned.1.call-start
  7.2 0.8 select_reduce_fusion
  8.1 0.2 convert_reduce_fusion.1
  8.3 0.2 compare_reduce_fusion
  9.1 0.2 convert_reduce_fusion
  9.3 0.7 stack.14
  10.0 0.2 multiply_reduce_fusion
  10.2 0.6 slice_bitcast_fusion
  10.8 0.6 convert_element_type.44.has_ref
  11.4 0.5 add_maximum_fusion.last_ref
  11.9 0.6 compare_convert_fusion.keep_ref
  12.5 0.0 copy-done
  12.5 0.9 fusion.1.crow_ref
  13.4 114.8 %shard_map.112 = (f32[1024,256]{1,0:T(8,128)}, f32[64,128,256]{2,1,0:T(8,128)}, f32[128,256]{1,0:T(8,128)}) custom-call(s32[128]{0:T(128)} %get-tuple-element.15.place_ref, s32[128]{0:T(128)} %get-tuple-element.14.user_ref, s32[128]{0:T(128)} %get-tuple-element.13.perm_ref, f32[128]{0:T(128)} %get-tuple-element.12.live_ref, ...), custom_call_target="tpu_custom_call" | custom-call | flops 10000000000 | bytes 20000000 | tf_op jit(solution)/shard_map/pallas_call | solution.py:324
  128.1 0.0 copy-start.1
  128.1 2.1 fusion
  130.2 0.0 all-reduce.2.cloned.1.call-update
  130.2 0.0 reduce-scatter.2.cloned.1.call-start
  130.3 0.7 reduce-scatter.2.cloned.1.call-update
  131.0 99.5 %all-reduce.2.cloned.1.call-done = f32[256,256]{1,0:T(8,128)} async-done(((f32[256,256]{1,0:T(8,128)}), f32[256,256]{1,0:T(8,128)}) %all-reduce.2.cloned.1.call-update) | async-done | bytes 262160 | tf_op jit(solution)/shard_map/psum | solution.py:371
  230.5 97.0 %reduce-scatter.2.cloned.1.call-done = f32[2,128,256]{2,1,0:T(8,128)} async-done(((f32[64,128,256]{2,1,0:T(8,128)}), f32[2,128,256]{2,1,0:T(8,128)}) %reduce-scatter.2.cloned.1.call-update) | async-done | bytes 262160 | tf_op jit(solution)/shard_map/reduce_scatter | solution.py:369
  327.5 0.0 copy-done.1
  327.5 1.0 copy.15
  328.5 1.7 copy.16
  (7 shorter events, 0.1 us)
Async XLA Ops:
  7.2 5.3 %copy-start = (bf16[256,256]{1,0:T(8,128)(2,1)S(1)}, bf16[256,256]{1,0:T(8,128)(2,1)}, u32[]{:S(2)}) copy-start(bf16[256,256]{1,0:T(8,128)(2,1)} %param.11) | copy-start | bytes 393220
  7.2 223.3 %all-reduce.2.cloned.1.call-start = ((), (), s32[]{:S(2)}) async-start(), calls=%async_computation.2 | async-start | bytes 524288 | tf_op jit(solution)/shard_map/psum | solution.py:371
  128.1 199.4 %copy-start.1 = (f32[1024,256]{1,0:T(8,128)S(1)}, f32[1024,256]{1,0:T(8,128)}, u32[]{:S(2)}) copy-start(f32[1024,256]{1,0:T(8,128)} %get-tuple-element.19) | copy-start | bytes 3145732
  130.2 197.3 %reduce-scatter.2.cloned.1.call-start = ((), (), s32[]{:S(2)}) async-start(), calls=%async_computation.1 | async-start | bytes 8650752 | tf_op jit(solution)/shard_map/reduce_scatter | solution.py:369
Sparse Core Ops, SparseCore 0:
  130.3 100.1 all-reduce.1
  235.2 92.2 reduce-scatter.1

commit v2 on v1

--- a/solution.py
+++ b/solution.py
@@ -14,25 +14,23 @@
 PER = 4
 SIDE = 128
 WIDTH = 256
+ROWS_A = 96
+PLACE, USER, PERM, LIVE, CTXT, KEEP, LAST, HAS = range(8)
 
 
 def kernel(
-    place_ref,
-    user_ref,
-    perm_ref,
-    live_ref,
-    keep_ref,
-    last_ref,
-    has_ref,
+    meta_ref,
     users_ref,
     shard_ref,
-    crow_ref,
+    context_ref,
+    ids_ref,
     mask_hbm,
     ugrad_ref,
-    ipart_ref,
-    cterm_ref,
+    igrad_ref,
+    cgrad_ref,
     items,
     mask,
+    ctx32,
     part,
     send1,
     recv1,
@@ -43,11 +41,30 @@
     segs,
     ahot,
     icb,
+    cterm,
+    call,
+    idall,
+    chot,
+    xs,
+    xr,
+    r1a,
+    r1ra,
+    r1b,
+    r1rb,
+    acc,
+    r2a,
+    r2ra,
+    r2b,
+    r2rb,
     mask_sem,
     ag_send,
     ag_recv,
     z_send,
     z_recv,
+    c_send,
+    c_recv,
+    r_send,
+    r_recv,
 ):
     z = lax.axis_index("rank")
     t = lax.axis_index("tiles")
@@ -98,6 +115,7 @@
     ag(0, blk(c, s, f), 2, dev(f + 1, s), shard_ref)
     ag(1, blk(c, s, f), 2, dev(f - 1, s), shard_ref)
     items[pl.ds(blk(c, s, f), 2)] = shard_ref[...]
+    ctx32[...] = context_ref[...].astype(F32)
     got(0, blk(c, s, f - 1), 2)
     ag(2, blk(c, s, f - 1), 1, dev(f + 1, s))
     got(1, blk(c, s, f + 1), 2)
@@ -167,8 +185,8 @@
             rcopy(views[d], views[d], z_send.at[ph, j, d], z_recv.at[ph, j, d], right).wait_recv()
 
     def item_context(p):
-        it = items[place_ref[p]].astype(F32)
-        return (it * crow_ref[pl.ds(p, 1), :]).astype(BF16)
+        it = items[meta_ref[PLACE, p]].astype(F32)
+        return (it * ctx32[pl.ds(meta_ref[CTXT, p], 1), :]).astype(BF16)
 
     def predict(j):
         slot = lax.rem(j, 4)
@@ -177,7 +195,7 @@
             o, k = n // PER, lax.rem(n, PER)
             p = j * 16 + n
             pr = lax.dot_general(
-                users_ref[user_ref[p]], item_context(p), (((1,), (1,)), ((), ())), preferred_element_type=F32
+                users_ref[meta_ref[USER, p]], item_context(p), (((1,), (1,)), ((), ())), preferred_element_type=F32
             )
             part[slot, o, k] = pr
             return 0
@@ -204,8 +222,8 @@
         for k in range(PER):
             p = j * 16 + z * PER + k
             pr = part[slot, z, k] + recv2[j, 0, k].astype(F32) + recv2[j, 1, k].astype(F32)
-            m = mask[perm_ref[p]].astype(F32)
-            resid[j, z, k] = (live_ref[p] * (1.0 + 4.0 * m) * (pr - m) * (1.0 / 128.0)).astype(BF16)
+            m = mask[meta_ref[PERM, p]].astype(F32)
+            resid[j, z, k] = (meta_ref[LIVE, p].astype(F32) * (1.0 + 4.0 * m) * (pr - m) * (1.0 / 128.0)).astype(BF16)
         for cp in zcopies(2, j):
             cp.start()
 
@@ -221,15 +239,15 @@
             for k in range(PER):
                 p = j * 16 + o * PER + k
                 r = resid[j, o, k]
-                u = user_ref[p]
+                u = meta_ref[USER, p]
                 for b in range(8):
                     ahot[pl.ds(b * SIDE, SIDE), pl.ds(k * SIDE, SIDE)] = jnp.where(u == b, r, jnp.zeros_like(r))
-                it = items[place_ref[p]].astype(F32)
-                cr = crow_ref[pl.ds(p, 1), :]
+                it = items[meta_ref[PLACE, p]].astype(F32)
+                cr = ctx32[pl.ds(meta_ref[CTXT, p], 1), :]
                 icb[pl.ds(k * SIDE, SIDE), :] = (it * cr).astype(BF16)
                 q = lax.dot_general(r, users_ref[u], (((0,), (0,)), ((), ())), preferred_element_type=F32)
-                cterm_ref[pl.ds(p, 1), :] = jnp.sum(it * q, axis=0, keepdims=True)
-                total = run[...] * keep_ref[p] + q * cr
+                cterm[pl.ds(p, 1), :] = jnp.sum(it * q, axis=0, keepdims=True)
+                total = run[...] * meta_ref[KEEP, p].astype(F32) + q * cr
                 run[...] = total
                 segs[p] = total.astype(BF16)
             ugrad_ref[...] += jnp.dot(ahot[...], icb[...], preferred_element_type=F32)
@@ -237,7 +255,78 @@
 
         lax.fori_loop(0, 4, group, 0)
 
+    def ccopies(g, k, arriving):
+        rows = pl.ds(0, ROWS_A) if g == 0 else pl.ds(ROWS_A, SIDE - ROWS_A)
+        pos = lambda ci, si, fi: (ci * 4 + lax.rem(si + 4, 4)) * 4 + lax.rem(fi + 4, 4)
+        start, count, to = (
+            (pos(c, s, f), 1, dev(f + 1, s)),
+            (pos(c, s, f), 1, dev(f - 1, s)),
+            (pos(c, s, f - 1), 1, dev(f + 1, s)),
+            (pos(c, s, 0 * f), 4, dev(f, s + 1)),
+            (pos(c, s, 0 * f), 4, dev(f, s - 1)),
+            (pos(c, s - 1, 0 * f), 4, dev(f, s + 1)),
+            (c * 16, 16, sib),
+        )[k]
+        into = (
+            pos(c, s, f - 1),
+            pos(c, s, f + 1),
+            pos(c, s, f + 2),
+            pos(c, s - 1, 0 * f),
+            pos(c, s + 1, 0 * f),
+            pos(c, s + 2, 0 * f),
+            (1 - c) * 16,
+        )[k]
+        at = into if arriving else start
+        views = [(call.at[pl.ds(at, count), rows], g)]
+        if g == 0:
+            views.append((idall.at[pl.ds(at, count)], 2))
+        return [rcopy(a, a, c_send.at[h, k], c_recv.at[h, k], to) for a, h in views]
+
+    def cstart(g, k):
+        for cp in ccopies(g, k, False):
+            cp.start()
+
+    def cwait(g, k):
+        for cp in ccopies(g, k, True):
+            cp.wait_recv()
+
+    def tick(g, n):
+        if n == 0:
+            own = (c * 4 + s) * 4 + f
+            if g == 0:
+                call[own, pl.ds(0, ROWS_A)] = cterm[pl.ds(0, ROWS_A), :].astype(BF16)
+                idall[own] = ids_ref[...]
+            else:
+                call[own, pl.ds(ROWS_A, SIDE - ROWS_A)] = cterm[pl.ds(ROWS_A, SIDE - ROWS_A), :].astype(BF16)
+            cstart(g, 0)
+            cstart(g, 1)
+        elif n == 1:
+            cwait(g, 0)
+            cstart(g, 2)
+            cwait(g, 1)
+        elif n == 2:
+            cwait(g, 2)
+            cstart(g, 3)
+            cstart(g, 4)
+        elif n == 3:
+            cwait(g, 3)
+            cstart(g, 5)
+            cwait(g, 4)
+        elif n == 4:
+            cwait(g, 5)
+            cstart(g, 6)
+        else:
+            cwait(g, 6)
+
     def step(i, _):
+        @pl.when(i == NB + 2)
+        def _():
+            tick(0, 1)
+
+        @pl.when(i == NB + 3)
+        def _():
+            tick(0, 3)
+
         @pl.when(i < NB)
         def _():
             predict(i)
@@ -258,17 +347,150 @@
         def _():
             gradients(i - 4)
 
+        @pl.when(i == NB + 1)
+        def _():
+            tick(0, 0)
+
+        @pl.when(i == NB + 2)
+        def _():
+            tick(0, 2)
+
+        @pl.when(i == NB + 3)
+        def _():
+            tick(0, 4)
+
         return 0
 
     lax.fori_loop(0, NB + 4, step, 0)
 
-    def finish(b, _):
-        ipart_ref[b] = segs[last_ref[b]].astype(F32) * has_ref[b]
+    def rc(k, src, dst, to):
+        return rcopy(src, dst, r_send.at[k], r_recv.at[k], to)
+
+    def rgot(k, dst):
+        rc(k, dst, dst, sib).wait_recv()
+
+    def own_sum(b):
+        return segs[meta_ref[LAST, b]].astype(F32) * meta_ref[HAS, b].astype(F32)
+
+    rcs = []
+
+    def rstart(k, src, dst, to):
+        cp = rc(k, src, dst, to)
+        cp.start()
+        rcs.append(cp)
+
+    for k, d in enumerate((2, 1, 3, 0)):
+        theirs = lax.rem(f + d, 4) * 8
+
+        def give(n, _):
+            xs[theirs + n] = own_sum((1 - c) * 32 + theirs + n).astype(BF16)
+            return 0
+
+        lax.fori_loop(0, 8, give, 0)
+        piece = pl.ds(theirs, 8)
+        rstart(k, xs.at[piece], xr.at[piece], sib)
+        if k == 0:
+            tick(1, 0)
+    tick(0, 5)
+
+    def hots(n, _):
+        ids = idall[n][0:1, :].astype(F32)
+        rows = lax.broadcasted_iota(jnp.int32, (WIDTH, SIDE), 0).astype(F32)
+        chot[n] = jnp.where(rows == ids, 1.0, 0.0).astype(BF16)
         return 0
 
-    lax.fori_loop(0, 64, finish, 0)
-    for cp in started:
+    lax.fori_loop(0, 32, hots, 0)
+
+    def chip_sum(si, n):
+        return own_sum(c * 32 + si * 8 + n) + xr[si * 8 + n].astype(F32)
+
+    def each(lo, hi, body):
+        def run_body(n, _):
+            body(n)
+            return 0
+
+        lax.fori_loop(lo, hi, run_body, 0)
+
+    far, hi, lo = lax.rem(s + 2, 4), lax.rem(s + 1, 4), lax.rem(s + 3, 4)
+    ahead, behind = dev(f, s + 1), dev(f, s - 1)
+
+    def put_far(n):
+        r1a[n] = chip_sum(far, n).astype(BF16)
+
+    rgot(0, xr.at[pl.ds(far * 8, 8)])
+    each(0, 8, put_far)
+    rstart(4, r1a.at[pl.ds(0, 4)], r1ra.at[0], ahead)
+    rstart(5, r1a.at[pl.ds(4, 4)], r1ra.at[1], behind)
+    tick(1, 1)
+
+    def put_hi(n):
+        r1b[0, n] = chip_sum(hi, n).astype(BF16)
+
+    def put_hi_more(n):
+        r1b[0, n] = (chip_sum(hi, n) + r1ra[0, n].astype(F32)).astype(BF16)
+
+    def put_lo(n):
+        r1b[1, n] = chip_sum(lo, n).astype(BF16)
+
+    def put_lo_more(n):
+        r1b[1, n] = (chip_sum(lo, n) + r1ra[1, n - 4].astype(F32)).astype(BF16)
+
+    rgot(1, xr.at[pl.ds(hi * 8, 8)])
+    each(4, 8, put_hi)
+    rgot(2, xr.at[pl.ds(lo * 8, 8)])
+    each(0, 4, put_lo)
+    rgot(4, r1ra.at[0])
+    each(0, 4, put_hi_more)
+    rstart(6, r1b.at[0], r1rb.at[0], ahead)
+    rgot(5, r1ra.at[1])
+    each(4, 8, put_lo_more)
+    rstart(7, r1b.at[1], r1rb.at[1], behind)
+    tick(1, 2)
+
+    def put_mine(n):
+        acc[n] = chip_sum(s, n)
+
+    def put_mine_more(n):
+        acc[n] += r1rb[0, n].astype(F32) + r1rb[1, n].astype(F32)
+
+    rgot(3, xr.at[pl.ds(s * 8, 8)])
+    each(0, 8, put_mine)
+    rgot(6, r1rb.at[0])
+    rgot(7, r1rb.at[1])
+    each(0, 8, put_mine_more)
+
+    far, hi, lo = lax.rem(f + 2, 4) * 2, lax.rem(f + 1, 4) * 2, lax.rem(f + 3, 4) * 2
+    ahead, behind = dev(f + 1, s), dev(f - 1, s)
+    r2a[...] = acc[pl.ds(far, 2)].astype(BF16)
+    rstart(8, r2a.at[0], r2ra.at[0], ahead)
+    rstart(9, r2a.at[1], r2ra.at[1], behind)
+    tick(1, 3)
+    r2b[0, 1] = acc[hi + 1].astype(BF16)
+    r2b[1, 0] = acc[lo].astype(BF16)
+    rgot(8, r2ra.at[0])
+    r2b[0, 0] = (acc[hi] + r2ra[0].astype(F32)).astype(BF16)
+    rstart(10, r2b.at[0], r2rb.at[0], ahead)
+    rgot(9, r2ra.at[1])
+    r2b[1, 1] = (acc[lo + 1] + r2ra[1].astype(F32)).astype(BF16)
+    rstart(11, r2b.at[1], r2rb.at[1], behind)
+    tick(1, 4)
+    rgot(10, r2rb.at[0])
+    rgot(11, r2rb.at[1])
+    igrad_ref[...] = acc[pl.ds(f * 2, 2)] + r2rb[0].astype(F32) + r2rb[1].astype(F32)
+    tick(1, 5)
+    cgrad_ref[...] = jnp.zeros_like(cgrad_ref)
+
+    def ctx_dot(n):
+        cgrad_ref[...] += jnp.dot(chot[n], call[n], preferred_element_type=F32)
+
+    each(0, 32, ctx_dot)
+
+    for cp in started + rcs:
         cp.wait_send()
+    for g in range(2):
+        for k in range(7):
+            for cp in ccopies(g, k, False):
+                cp.wait_send()
     for ph in range(4):
         def drain(j, _):
             for cp in zcopies(ph, j):
@@ -310,66 +532,78 @@
     live = (ids < tile_count[0]).astype(jnp.int32)
     vals = jnp.stack([place, tile_user, ids, live, tile_context])
     ordered = jnp.sum(pick[None] * vals[:, None, :], axis=2)
-    place_s, user_s, perm, live_s, ctx_s = (ordered[i] for i in range(5))
+    place_s, ctx_s = ordered[PLACE], ordered[CTXT]
     before = jnp.concatenate([jnp.full((1,), -1, jnp.int32), place_s[:-1]])
-    keep = (place_s == before).astype(F32)
-    ends = place_of(jnp.arange(nblocks, dtype=jnp.int32))
-    last = jnp.maximum(jnp.sum((place[None, :] <= ends[:, None]).astype(jnp.int32), axis=1) - 1, 0)
-    has = jnp.any(place[None, :] == ends[:, None], axis=1).astype(F32)
-    chot = ctx_s[:, None] == jnp.arange(nctx)[None, :]
-    crow = jnp.dot(chot.astype(BF16), context_factor, preferred_element_type=F32)
+    keep = (place_s == before).astype(jnp.int32)
+    last = jnp.maximum(jnp.sum((place[None, :] <= ids[:, None]).astype(jnp.int32), axis=1) - 1, 0)
+    has = jnp.any(place[None, :] == ids[:, None], axis=1).astype(jnp.int32)
+    meta = jnp.concatenate([ordered, jnp.stack([keep, last, has])])
+    ids16 = jnp.broadcast_to(ctx_s.astype(BF16)[None, :], (16, n))
     smem = pl.BlockSpec(memory_space=pltpu.SMEM)
     vmem = pl.BlockSpec(memory_space=pltpu.VMEM)
     tile2 = (SIDE, SIDE)
-    ugrad, ipart, cterm = pl.pallas_call(
+    wide = (SIDE, WIDTH)
+    ugrad, igrad, cgrad = pl.pallas_call(
         kernel,
         out_shape=(
             jax.ShapeDtypeStruct((1024, WIDTH), F32),
-            jax.ShapeDtypeStruct((nblocks, SIDE, WIDTH), F32),
-            jax.ShapeDtypeStruct((n, WIDTH), F32),
+            jax.ShapeDtypeStruct((2,) + wide, F32),
+            jax.ShapeDtypeStruct((nctx, WIDTH), F32),
         ),
-        in_specs=[smem] * 7 + [vmem] * 3 + [pl.BlockSpec(memory_space=pl.ANY)],
+        in_specs=[smem] + [vmem] * 4 + [pl.BlockSpec(memory_space=pl.ANY)],
         out_specs=(vmem,) * 3,
         scratch_shapes=[
-            pltpu.VMEM((64, SIDE, WIDTH), BF16),
+            pltpu.VMEM((64,) + wide, BF16),
             pltpu.VMEM((n,) + tile2, jnp.int32),
+            pltpu.VMEM((nctx, WIDTH), F32),
             pltpu.VMEM((4, 4, PER) + tile2, F32),
             pltpu.VMEM((NB, PER) + tile2, BF16),
             pltpu.VMEM((NB, 2, 2) + tile2, BF16),
             pltpu.VMEM((NB, 2, PER) + tile2, BF16),
             pltpu.VMEM((NB, 2, PER) + tile2, BF16),
             pltpu.VMEM((NB, 4, PER) + tile2, BF16),
-            pltpu.VMEM((SIDE, WIDTH), F32),
-            pltpu.VMEM((n, SIDE, WIDTH), BF16),
+            pltpu.VMEM(wide, F32),
+            pltpu.VMEM((n,) + wide, BF16),
             pltpu.VMEM((1024, PER * SIDE), BF16),
             pltpu.VMEM((PER * SIDE, WIDTH), BF16),
+            pltpu.VMEM(wide, F32),
+            pltpu.VMEM((32,) + wide, BF16),
+            pltpu.VMEM((32, 16, SIDE), BF16),
+            pltpu.VMEM((32, nctx, SIDE), BF16),
+            pltpu.VMEM((32,) + wide, BF16),
+            pltpu.VMEM((32,) + wide, BF16),
+            pltpu.VMEM((8,) + wide, BF16),
+            pltpu.VMEM((2, 4) + wide, BF16),
+            pltpu.VMEM((2, 8) + wide, BF16),
+            pltpu.VMEM((2, 8) + wide, BF16),
+            pltpu.VMEM((8,) + wide, F32),
+            pltpu.VMEM((2,) + wide, BF16),
+            pltpu.VMEM((2,) + wide, BF16),
+            pltpu.VMEM((2, 2) + wide, BF16),
+            pltpu.VMEM((2, 2) + wide, BF16),
             pltpu.SemaphoreType.DMA,
             pltpu.SemaphoreType.DMA((12,)),
             pltpu.SemaphoreType.DMA((12,)),
             pltpu.SemaphoreType.DMA((4, NB, 2)),
             pltpu.SemaphoreType.DMA((4, NB, 2)),
+            pltpu.SemaphoreType.DMA((3, 7)),
+            pltpu.SemaphoreType.DMA((3, 7)),
+            pltpu.SemaphoreType.DMA((12,)),
+            pltpu.SemaphoreType.DMA((12,)),
         ],
         compiler_params=pltpu.CompilerParams(
             collective_id=0, has_side_effects=True, vmem_limit_bytes=62 * 1024 * 1024
         ),
         cost_estimate=pl.CostEstimate(flops=10_000_000_000, bytes_accessed=20_000_000, transcendentals=0),
     )(
-        place_s,
-        user_s,
-        perm,
-        live_s.astype(F32),
-        keep,
-        last,
-        has,
+        meta,
         user_factor.reshape(-1, SIDE, WIDTH),
         item_factor.reshape(-1, SIDE, WIDTH),
-        crow,
+        context_factor,
+        ids16,
         tile_mask,
     )
-    item_grad = lax.psum_scatter(ipart, "tiles", scatter_dimension=0, tiled=True)
-    ctx_part = jnp.dot(chot.astype(F32).T, cterm, precision=lax.Precision.HIGHEST)
-    context_grad = lax.psum(ctx_part, "tiles")
-    return (ugrad, item_grad.reshape(-1, WIDTH), context_grad)
+    return (ugrad, igrad.reshape(-1, WIDTH), cgrad)
 
 
 def solution(mesh):

time: 337 us -> 164 us (0.49)
  waiting for transfers between devices: 197 us -> 0 us
  Pallas kernels: 115 us -> 153 us
  between operations: 14.8 us -> 1.33 us
  local copies, waits for them, and re-layouts: 3.35 us -> 6.9 us
    psum x1 -> x0, waiting for transfers between devices: 99.5 us -> none  [local(): context_grad = lax.psum(ctx_part, 'tiles')]
    reduce_scatter x1 -> x0, waiting for transfers between devices: 97 us -> none  [local(): lax.psum_scatter(ipart, 'tiles', scatter_dimension=0, tiled=True)]
    pallas_call x1, Pallas kernels: 115 us -> 153 us  [local(): pl.pallas_call(kernel, out_shape=(jax.ShapeDtypeStruct((1024, WIDTH), F32...]
  transfers between devices with their start and end apart: 2 -> 0, of which waited for: 2 -> 0; matrix products, arithmetic and copies ran while one was open for 0% -> 0% of each run, Pallas kernels for 0% -> 0%
where the time goes in v2:
time: 164 us; the launch traced here: 163 us
  Pallas kernels  153 us (93%)
  local copies, waits for them, and re-layouts  6.9 us (4%)
  other arithmetic  2 us (1%)
    pallas_call x1, Pallas kernels, local(): pl.pallas_call(kernel, out_shape=(jax.ShapeDtypeStruct((1024, WIDTH), F32...  153 us
    unnamed x3, local copies, waits for them, and re-layouts  5.6 us

profile of v2, /device:TPU:0, one launch (start us, length us, event | category | flops | bytes accessed | tf_op | source)
XLA Modules:
  0.0 163.4 jit_solution(13048855359127161765)
XLA Ops:
  1.3 0.8 select_reduce_fusion
  2.1 0.1 fusion.1
  2.3 0.2 convert_reduce_fusion
  2.4 0.7 stack.8
  3.1 0.2 multiply_reduce_fusion
  3.3 0.1 compare_convert_fusion
  3.4 0.6 pad_add_fusion.meta_ref
  4.0 0.6 broadcast_in_dim.5.ids_ref
  4.6 153.2 %shard_map.112 = (f32[1024,256]{1,0:T(8,128)}, f32[2,128,256]{2,1,0:T(8,128)}, f32[256,256]{1,0:T(8,128)}) custom-call(s32[8,128]{1,0:T(8,128)} %pad_add_fusion.meta_ref, bf16[8,128,256]{2,1,0:T(8,128)(2,1)} %bitcast.29, bf16[2,128,256]{2,1,0:T(8,128)(2,1)} %bitcast.30, bf16[256,256]{1,0:T(8,128)(2,1)} %context_ref.1, ...), custom_call_target="tpu_custom_call" | custom-call | flops 10000000000 | bytes 20000000 | tf_op jit(solution)/shard_map/pallas_call | solution.py:546
  157.8 2.3 %copy.16 = f32[1024,256]{1,0:T(8,128)} copy(f32[1024,256]{1,0:T(8,128)} %get-tuple-element.16) | data formatting | bytes 2097152
  160.0 1.7 %copy.17 = f32[256,256]{1,0:T(8,128)} copy(f32[256,256]{1,0:T(8,128)} %bitcast.26) | data formatting | bytes 524288
  161.7 1.7 %copy.18 = f32[256,256]{1,0:T(8,128)} copy(f32[256,256]{1,0:T(8,128)} %get-tuple-element.18) | data formatting | bytes 524288
  (10 shorter events, 0.1 us)

commit v3 on v1

--- a/solution.py
+++ b/solution.py
@@ -14,25 +14,24 @@
 PER = 4
 SIDE = 128
 WIDTH = 256
+ROWS_B = 32
+ROWS_A = SIDE - ROWS_B
+PLACE, USER, PERM, LIVE, CTXT, KEEP, LAST, HAS = range(8)
 
 
 def kernel(
-    place_ref,
-    user_ref,
-    perm_ref,
-    live_ref,
-    keep_ref,
-    last_ref,
-    has_ref,
+    meta_ref,
     users_ref,
     shard_ref,
-    crow_ref,
+    context_ref,
+    ids_ref,
     mask_hbm,
     ugrad_ref,
-    ipart_ref,
-    cterm_ref,
+    igrad_ref,
+    cgrad_ref,
     items,
     mask,
+    ctx32,
     part,
     send1,
     recv1,
@@ -43,11 +42,27 @@
     segs,
     ahot,
     icb,
+    cterm,
+    call_a,
+    call_b,
+    idall,
+    chot_a,
+    chot_b,
+    xs,
+    xr,
+    r1s,
+    r1r,
+    r2s,
+    r2r,
     mask_sem,
     ag_send,
     ag_recv,
     z_send,
     z_recv,
+    c_send,
+    c_recv,
+    r_send,
+    r_recv,
 ):
     z = lax.axis_index("rank")
     t = lax.axis_index("tiles")
@@ -67,7 +82,10 @@
         return {"rank": lax.rem(z + d + 4, 4), "tiles": t}
 
     sib = {"rank": z, "tiles": t + 1 - 2 * c}
-    partners = (dev(f + 1, s), dev(f - 1, s), dev(f, s + 1), dev(f, s - 1), devz(1), devz(-1), sib)
+    turns = (1, 3, 2)
+    fpeer = {d: dev(f + d, s) for d in turns}
+    speer = {d: dev(f, s + d) for d in turns}
+    partners = tuple(fpeer.values()) + tuple(speer.values()) + (devz(1), devz(-1), sib)
     mask_copy = pltpu.make_async_copy(mask_hbm, mask, mask_sem)
     mask_copy.start()
     barrier = pltpu.get_barrier_semaphore()
@@ -82,6 +100,9 @@
 
     started = []
 
+    def blk(ci, si, fi):
+        return ((ci * 4 + lax.rem(si + 4, 4)) * 4 + lax.rem(fi + 4, 4)) * 2
+
     def ag(k, start, size, to, src=None):
         view = items.at[pl.ds(start, size)]
         cp = rcopy(view if src is None else src, view, ag_send.at[k], ag_recv.at[k], to)
@@ -92,39 +113,29 @@
         view = items.at[pl.ds(start, size)]
         rcopy(view, view, ag_send.at[k], ag_recv.at[k], sib).wait_recv()
 
-    def blk(ci, si, fi):
-        return ((ci * 4 + lax.rem(si + 4, 4)) * 4 + lax.rem(fi + 4, 4)) * 2
-
-    ag(0, blk(c, s, f), 2, dev(f + 1, s), shard_ref)
-    ag(1, blk(c, s, f), 2, dev(f - 1, s), shard_ref)
-    items[pl.ds(blk(c, s, f), 2)] = shard_ref[...]
-    got(0, blk(c, s, f - 1), 2)
-    ag(2, blk(c, s, f - 1), 1, dev(f + 1, s))
-    got(1, blk(c, s, f + 1), 2)
-    ag(3, blk(c, s, f + 1) + 1, 1, dev(f - 1, s))
-    got(2, blk(c, s, f + 2), 1)
-    got(3, blk(c, s, f + 2) + 1, 1)
-    slab = lambda si: blk(c, si, f * 0)
-    other = lambda si: blk(1 - c, si, f * 0)
-    ag(4, slab(s), 8, dev(f, s + 1))
-    ag(5, slab(s), 8, dev(f, s - 1))
-    ag(6, slab(s), 8, sib)
-    got(4, slab(s - 1), 8)
-    ag(7, slab(s - 1), 4, dev(f, s + 1))
-    ag(8, slab(s - 1), 8, sib)
-    got(5, slab(s + 1), 8)
-    ag(9, slab(s + 1) + 4, 4, dev(f, s - 1))
-    ag(10, slab(s + 1), 8, sib)
-    got(7, slab(s + 2), 4)
-    got(9, slab(s + 2) + 4, 4)
-    ag(11, slab(s + 2), 8, sib)
-    got(6, other(f), 8)
-    got(8, other(f - 1), 8)
-    got(10, other(f + 1), 8)
-    got(11, other(f + 2), 8)
-    mask_copy.wait()
+    mine = blk(c, s, f)
+    for d in turns:
+        ag(d, mine, 2, fpeer[d], shard_ref)
+    for d in turns:
+        ag(4 + d, mine, 2, speer[d], shard_ref)
+    items[pl.ds(mine, 2)] = shard_ref[...]
+    ctx32[...] = context_ref[...].astype(F32)
     ugrad_ref[...] = jnp.zeros_like(ugrad_ref)
     run[...] = jnp.zeros_like(run)
+    call_a[...] = jnp.zeros_like(call_a)
+    for d in turns:
+        e = 4 - d
+        got(d, blk(c, s, f + e), 2)
+        for dd in turns:
+            ag(4 + 4 * e + dd, blk(c, s, f + e), 2, speer[dd])
+    ag(20, blk(c, s, 0 * f), 8, sib)
+    for d in turns:
+        for e in (0, 3, 1, 2):
+            got(4 + 4 * e + d, blk(c, s - d, f + e), 2)
+        ag(20 + d, blk(c, s - d, 0 * f), 8, sib)
+    for d in (0, 1, 3, 2):
+        got(20 + d, blk(1 - c, f - d, 0 * f), 8)
+    mask_copy.wait()
 
     right, left = devz(1), devz(-1)
 
@@ -167,8 +178,8 @@
             rcopy(views[d], views[d], z_send.at[ph, j, d], z_recv.at[ph, j, d], right).wait_recv()
 
     def item_context(p):
-        it = items[place_ref[p]].astype(F32)
-        return (it * crow_ref[pl.ds(p, 1), :]).astype(BF16)
+        it = items[meta_ref[PLACE, p]].astype(F32)
+        return (it * ctx32[pl.ds(meta_ref[CTXT, p], 1), :]).astype(BF16)
 
     def predict(j):
         slot = lax.rem(j, 4)
@@ -177,7 +188,7 @@
             o, k = n // PER, lax.rem(n, PER)
             p = j * 16 + n
             pr = lax.dot_general(
-                users_ref[user_ref[p]], item_context(p), (((1,), (1,)), ((), ())), preferred_element_type=F32
+                users_ref[meta_ref[USER, p]], item_context(p), (((1,), (1,)), ((), ())), preferred_element_type=F32
             )
             part[slot, o, k] = pr
             return 0
@@ -204,8 +215,8 @@
         for k in range(PER):
             p = j * 16 + z * PER + k
             pr = part[slot, z, k] + recv2[j, 0, k].astype(F32) + recv2[j, 1, k].astype(F32)
-            m = mask[perm_ref[p]].astype(F32)
-            resid[j, z, k] = (live_ref[p] * (1.0 + 4.0 * m) * (pr - m) * (1.0 / 128.0)).astype(BF16)
+            m = mask[meta_ref[PERM, p]].astype(F32)
+            resid[j, z, k] = (meta_ref[LIVE, p].astype(F32) * (1.0 + 4.0 * m) * (pr - m) * (1.0 / 128.0)).astype(BF16)
         for cp in zcopies(2, j):
             cp.start()
 
@@ -221,15 +232,15 @@
             for k in range(PER):
                 p = j * 16 + o * PER + k
                 r = resid[j, o, k]
-                u = user_ref[p]
+                u = meta_ref[USER, p]
                 for b in range(8):
                     ahot[pl.ds(b * SIDE, SIDE), pl.ds(k * SIDE, SIDE)] = jnp.where(u == b, r, jnp.zeros_like(r))
-                it = items[place_ref[p]].astype(F32)
-                cr = crow_ref[pl.ds(p, 1), :]
+                it = items[meta_ref[PLACE, p]].astype(F32)
+                cr = ctx32[pl.ds(meta_ref[CTXT, p], 1), :]
                 icb[pl.ds(k * SIDE, SIDE), :] = (it * cr).astype(BF16)
                 q = lax.dot_general(r, users_ref[u], (((0,), (0,)), ((), ())), preferred_element_type=F32)
-                cterm_ref[pl.ds(p, 1), :] = jnp.sum(it * q, axis=0, keepdims=True)
-                total = run[...] * keep_ref[p] + q * cr
+                cterm[pl.ds(p, 1), :] = jnp.sum(it * q, axis=0, keepdims=True)
+                total = run[...] * meta_ref[KEEP, p].astype(F32) + q * cr
                 run[...] = total
                 segs[p] = total.astype(BF16)
             ugrad_ref[...] += jnp.dot(ahot[...], icb[...], preferred_element_type=F32)
@@ -237,7 +248,63 @@
 
         lax.fori_loop(0, 4, group, 0)
 
+    def ccopies(g, k, arriving):
+        pos = lambda si, fi: (c * 4 + lax.rem(si + 4, 4)) * 4 + lax.rem(fi + 4, 4)
+        if k < 4:
+            at, count, to = (pos(s, f - k) if arriving else pos(s, f)), 1, fpeer[k]
+        elif k < 8:
+            at, count, to = (pos(s - (k - 4), 0 * f) if arriving else pos(s, 0 * f)), 4, speer[k - 4]
+        else:
+            at, count, to = ((1 - c) * 16 if arriving else c * 16), 16, sib
+        if g == 0:
+            a = call_a.at[pl.ds(at, count), pl.ds(0, ROWS_A)]
+        else:
+            a = (call_b if g == 1 else idall).at[pl.ds(at, count)]
+        return rcopy(a, a, c_send.at[g, k], c_recv.at[g, k], to)
+
+    def tick(g, n):
+        own = (c * 4 + s) * 4 + f
+        if n == 0:
+            if g == 0:
+                call_a[own, pl.ds(0, ROWS_A)] = cterm[pl.ds(0, ROWS_A), :].astype(BF16)
+            elif g == 1:
+                call_b[own] = cterm[pl.ds(ROWS_A, ROWS_B), :].astype(BF16)
+            else:
+                row = lax.broadcasted_iota(jnp.int32, (16, SIDE), 0)
+                lane = lax.broadcasted_iota(jnp.int32, (16, SIDE), 1)
+                hidden = (row == 1) & (lane // ROWS_B != f)
+                idall[own] = jnp.where(hidden, 0.0, ids_ref[...].astype(F32)).astype(BF16)
+        else:
+            for d in turns if n < 3 else (0,):
+                ccopies(g, 4 * (n - 1) + d, True).wait_recv()
+        if n < 3:
+            for d in turns if n < 2 else (0,):
+                ccopies(g, 4 * n + d, False).start()
+
+    def hot(ids):
+        rows = lax.broadcasted_iota(jnp.int32, (WIDTH, SIDE), 0).astype(F32)
+        return jnp.where(rows == ids, 1.0, 0.0).astype(BF16)
+
+    def hots(n, _):
+        rest = jnp.zeros((1, SIDE), F32)
+        for k in range(4):
+            both = idall[n * 4 + k].astype(F32)
+            chot_a[n * 4 + k] = hot(both[0:1, :])
+            rest += both[1:2, :]
+        chot_b[n] = hot(rest)
+        return 0
+
     def step(i, _):
+        for n in range(4):
+
+            @pl.when(i == 2 + n)
+            def _():
+                tick(2, n)
+
+        @pl.when(i == NB + 3)
+        def _():
+            tick(0, 2)
+
         @pl.when(i < NB)
         def _():
             predict(i)
@@ -258,17 +325,100 @@
         def _():
             gradients(i - 4)
 
+        @pl.when(i == NB + 1)
+        def _():
+            lax.fori_loop(0, 8, hots, 0)
+            tick(0, 0)
+
+        @pl.when(i == NB + 2)
+        def _():
+            tick(0, 1)
+
         return 0
 
     lax.fori_loop(0, NB + 4, step, 0)
 
-    def finish(b, _):
-        ipart_ref[b] = segs[last_ref[b]].astype(F32) * has_ref[b]
+    def rc(k, src, dst, to):
+        return rcopy(src, dst, r_send.at[k], r_recv.at[k], to)
+
+    def rgot(k, dst):
+        rc(k, dst, dst, sib).wait_recv()
+
+    def own_sum(b):
+        v = segs[meta_ref[LAST, b]]
+        return jnp.where(meta_ref[HAS, b] > 0, v, jnp.zeros_like(v))
+
+    rcs = []
+
+    def rstart(k, src, dst, to):
+        cp = rc(k, src, dst, to)
+        cp.start()
+        rcs.append(cp)
+
+    order = (1, 3, 2, 0)
+    for d in order:
+        theirs = lax.rem(s + d, 4)
+
+        def give(n, _):
+            xs[theirs * 8 + n] = own_sum(blk(1 - c, n // 2, theirs) + lax.rem(n, 2))
+            return 0
+
+        lax.fori_loop(0, 8, give, 0)
+        piece = pl.ds(theirs * 8, 8)
+        rstart(d, xs.at[piece], xr.at[piece], sib)
+        if d == 1:
+            tick(1, 0)
+
+    def chip_sum(si, fi, h):
+        return own_sum(blk(c, si, fi) + h).astype(F32) + xr[lax.rem(fi, 4) * 8 + lax.rem(si, 4) * 2 + h].astype(F32)
+
+    for d in order:
+        fi = lax.rem(f + d, 4)
+        rgot(d, xr.at[pl.ds(fi * 8, 8)])
+        for e in (2, 1, 3):
+            for h in range(2):
+                r1s[d, e, h] = chip_sum(s + e, fi, h).astype(BF16)
+            rstart(4 + 4 * d + e, r1s.at[d, e], r1r.at[d, e], speer[e])
+    tick(1, 1)
+    tick(0, 3)
+    cgrad_ref[...] = jnp.zeros_like(cgrad_ref)
+
+    def ctx_dot(n, _):
+        cgrad_ref[...] += jnp.dot(chot_a[n], call_a[n], preferred_element_type=F32)
         return 0
 
-    lax.fori_loop(0, 64, finish, 0)
-    for cp in started:
+    def plane_sum(d, h):
+        total = chip_sum(s, f + d, h)
+        for e in turns:
+            total += r1r[d, e, h].astype(F32)
+        return total
+
+    for d in order:
+        for e in turns:
+            rgot(4 + 4 * d + e, r1r.at[d, e])
+        for h in range(2):
+            if d:
+                r2s[d, h] = plane_sum(d, h).astype(BF16)
+            else:
+                igrad_ref[pl.ds(h * SIDE, SIDE), :] = plane_sum(d, h)
+        if d:
+            rstart(20 + d, r2s.at[d], r2r.at[d], fpeer[d])
+        if d == 1:
+            tick(1, 2)
+            lax.fori_loop(0, 32, ctx_dot, 0)
+    tick(1, 3)
+    for n in range(8):
+        rows = call_b[pl.ds(4 * n, 4)].reshape(SIDE, WIDTH)
+        cgrad_ref[...] += jnp.dot(chot_b[n], rows, preferred_element_type=F32)
+    for d in turns:
+        rgot(20 + d, r2r.at[d])
+        igrad_ref[...] += r2r[d].reshape(2 * SIDE, WIDTH).astype(F32)
+
+    for cp in started + rcs:
         cp.wait_send()
+    for g in range(3):
+        for k in (1, 2, 3, 5, 6, 7, 8):
+            ccopies(g, k, False).wait_send()
     for ph in range(4):
         def drain(j, _):
             for cp in zcopies(ph, j):
@@ -276,6 +426,17 @@
             return 0
 
         lax.fori_loop(0, NB, drain, 0)
+
+
+def hand_over(a_ref, b_ref, c_ref, a_out, b_out, c_out, sem):
+    copies = [
+        pltpu.make_async_copy(src, dst, sem.at[k])
+        for k, (src, dst) in enumerate(((a_ref, a_out), (b_ref, b_out), (c_ref, c_out)))
+    ]
+    for cp in copies:
+        cp.start()
+    for cp in copies:
+        cp.wait()
 
 
 def local(
@@ -310,66 +471,83 @@
     live = (ids < tile_count[0]).astype(jnp.int32)
     vals = jnp.stack([place, tile_user, ids, live, tile_context])
     ordered = jnp.sum(pick[None] * vals[:, None, :], axis=2)
-    place_s, user_s, perm, live_s, ctx_s = (ordered[i] for i in range(5))
+    place_s, ctx_s = ordered[PLACE], ordered[CTXT]
     before = jnp.concatenate([jnp.full((1,), -1, jnp.int32), place_s[:-1]])
-    keep = (place_s == before).astype(F32)
-    ends = place_of(jnp.arange(nblocks, dtype=jnp.int32))
-    last = jnp.maximum(jnp.sum((place[None, :] <= ends[:, None]).astype(jnp.int32), axis=1) - 1, 0)
-    has = jnp.any(place[None, :] == ends[:, None], axis=1).astype(F32)
-    chot = ctx_s[:, None] == jnp.arange(nctx)[None, :]
-    crow = jnp.dot(chot.astype(BF16), context_factor, preferred_element_type=F32)
+    keep = (place_s == before).astype(jnp.int32)
+    last = jnp.maximum(jnp.sum((place[None, :] <= ids[:, None]).astype(jnp.int32), axis=1) - 1, 0)
+    has = jnp.any(place[None, :] == ids[:, None], axis=1).astype(jnp.int32)
+    meta = jnp.concatenate([ordered, jnp.stack([keep, last, has])])
+    rows = jnp.stack([ctx_s, jnp.tile(ctx_s[ROWS_A:], n // ROWS_B)])
+    ids16 = jnp.pad(rows, ((0, 14), (0, 0))).astype(BF16)
     smem = pl.BlockSpec(memory_space=pltpu.SMEM)
     vmem = pl.BlockSpec(memory_space=pltpu.VMEM)
     tile2 = (SIDE, SIDE)
-    ugrad, ipart, cterm = pl.pallas_call(
+    wide = (SIDE, WIDTH)
+    ugrad, igrad, cgrad = pl.pallas_call(
         kernel,
         out_shape=(
             jax.ShapeDtypeStruct((1024, WIDTH), F32),
-            jax.ShapeDtypeStruct((nblocks, SIDE, WIDTH), F32),
-            jax.ShapeDtypeStruct((n, WIDTH), F32),
+            jax.ShapeDtypeStruct((2 * SIDE, WIDTH), F32),
+            jax.ShapeDtypeStruct((nctx, WIDTH), F32),
         ),
-        in_specs=[smem] * 7 + [vmem] * 3 + [pl.BlockSpec(memory_space=pl.ANY)],
+        in_specs=[smem] + [vmem] * 4 + [pl.BlockSpec(memory_space=pl.ANY)],
         out_specs=(vmem,) * 3,
         scratch_shapes=[
-            pltpu.VMEM((64, SIDE, WIDTH), BF16),
+            pltpu.VMEM((64,) + wide, BF16),
             pltpu.VMEM((n,) + tile2, jnp.int32),
+            pltpu.VMEM((nctx, WIDTH), F32),
             pltpu.VMEM((4, 4, PER) + tile2, F32),
             pltpu.VMEM((NB, PER) + tile2, BF16),
             pltpu.VMEM((NB, 2, 2) + tile2, BF16),
             pltpu.VMEM((NB, 2, PER) + tile2, BF16),
             pltpu.VMEM((NB, 2, PER) + tile2, BF16),
             pltpu.VMEM((NB, 4, PER) + tile2, BF16),
-            pltpu.VMEM((SIDE, WIDTH), F32),
-            pltpu.VMEM((n, SIDE, WIDTH), BF16),
+            pltpu.VMEM(wide, F32),
+            pltpu.VMEM((n,) + wide, BF16),
             pltpu.VMEM((1024, PER * SIDE), BF16),
             pltpu.VMEM((PER * SIDE, WIDTH), BF16),
+            pltpu.VMEM(wide, F32),
+            pltpu.VMEM((32,) + wide, BF16),
+            pltpu.VMEM((32, 32, WIDTH), BF16),
+            pltpu.VMEM((32, 16, SIDE), BF16),
+            pltpu.VMEM((32, nctx, SIDE), BF16),
+            pltpu.VMEM((8, nctx, SIDE), BF16),
+            pltpu.VMEM((32,) + wide, BF16),
+            pltpu.VMEM((32,) + wide, BF16),
+            pltpu.VMEM((4, 4, 2) + wide, BF16),
+            pltpu.VMEM((4, 4, 2) + wide, BF16),
+            pltpu.VMEM((4, 2) + wide, BF16),
+            pltpu.VMEM((4, 2) + wide, BF16),
             pltpu.SemaphoreType.DMA,
-            pltpu.SemaphoreType.DMA((12,)),
-            pltpu.SemaphoreType.DMA((12,)),
+            pltpu.SemaphoreType.DMA((24,)),
+            pltpu.SemaphoreType.DMA((24,)),
             pltpu.SemaphoreType.DMA((4, NB, 2)),
             pltpu.SemaphoreType.DMA((4, NB, 2)),
+            pltpu.SemaphoreType.DMA((3, 9)),
+            pltpu.SemaphoreType.DMA((3, 9)),
+            pltpu.SemaphoreType.DMA((24,)),
+            pltpu.SemaphoreType.DMA((24,)),
         ],
         compiler_params=pltpu.CompilerParams(
             collective_id=0, has_side_effects=True, vmem_limit_bytes=62 * 1024 * 1024
         ),
         cost_estimate=pl.CostEstimate(flops=10_000_000_000, bytes_accessed=20_000_000, transcendentals=0),
     )(
-        place_s,
-        user_s,
-        perm,
-        live_s.astype(F32),
-        keep,
-        last,
-        has,
+        meta,
         user_factor.reshape(-1, SIDE, WIDTH),
         item_factor.reshape(-1, SIDE, WIDTH),
-        crow,
+        context_factor,
+        ids16,
         tile_mask,
     )
-    item_grad = lax.psum_scatter(ipart, "tiles", scatter_dimension=0, tiled=True)
-    ctx_part = jnp.dot(chot.astype(F32).T, cterm, precision=lax.Precision.HIGHEST)
-    context_grad = lax.psum(ctx_part, "tiles")
-    return (ugrad, item_grad.reshape(-1, WIDTH), context_grad)
+    anywhere = pl.BlockSpec(memory_space=pl.ANY)
+    return pl.pallas_call(
+        hand_over,
+        out_shape=tuple(jax.ShapeDtypeStruct(a.shape, a.dtype) for a in (ugrad, igrad, cgrad)),
+        in_specs=[anywhere] * 3,
+        out_specs=(anywhere,) * 3,
+        scratch_shapes=[pltpu.SemaphoreType.DMA((3,))],
+    )(ugrad, igrad, cgrad)
 
 
 def solution(mesh):

time: 337 us -> 201 us (0.60)
  waiting for transfers between devices: 197 us -> 0 us
  Pallas kernels: 115 us -> 196 us
  between operations: 14.8 us -> 1.33 us
    psum x1 -> x0, waiting for transfers between devices: 99.5 us -> none  [local(): context_grad = lax.psum(ctx_part, 'tiles')]
    reduce_scatter x1 -> x0, waiting for transfers between devices: 97 us -> none  [local(): lax.psum_scatter(ipart, 'tiles', scatter_dimension=0, tiled=True)]
    pallas_call x0 -> x1, Pallas kernels: none -> 48.8 us  [local(): pl.pallas_call(hand_over, out_shape=tuple((jax.ShapeDtypeStruct(a.shape,...]
    pallas_call x1, Pallas kernels: 115 us -> 147 us  [local(): pl.pallas_call(kernel, out_shape=(jax.ShapeDtypeStruct((1024, WIDTH), F32...]
  transfers between devices with their start and end apart: 2 -> 0, of which waited for: 2 -> 0; matrix products, arithmetic and copies ran while one was open for 0% -> 0% of each run, Pallas kernels for 0% -> 0%
where the time goes in v3:
time: 201 us; the launch traced here: 200 us
  Pallas kernels  196 us (98%)
  other arithmetic  2.68 us (1%)
    pallas_call x1, Pallas kernels, local(): pl.pallas_call(kernel, out_shape=(jax.ShapeDtypeStruct((1024, WIDTH), F32...  147 us
    pallas_call x1, Pallas kernels, local(): pl.pallas_call(hand_over, out_shape=tuple((jax.ShapeDtypeStruct(a.shape,...  48.8 us

profile of v3, /device:TPU:0, one launch (start us, length us, event | category | flops | bytes accessed | tf_op | source)
XLA Modules:
  0.0 200.3 jit_solution(11975169876397381049)
XLA Ops:
  1.3 0.8 select_reduce_fusion
  2.1 0.1 fusion.1
  2.3 0.2 convert_reduce_fusion
  2.4 0.7 stack.21
  3.1 0.2 multiply_reduce_fusion
  3.3 0.1 convert_bitcast_fusion
  3.4 0.1 stack_tile.4
  3.5 0.1 compare_convert_fusion
  3.6 0.6 pad_add_fusion.meta_ref
  4.2 0.6 fusion.4.ids_ref
  4.8 146.8 %shard_map.112 = (f32[1024,256]{1,0:T(8,128)}, f32[256,256]{1,0:T(8,128)}, f32[256,256]{1,0:T(8,128)}) custom-call(s32[8,128]{1,0:T(8,128)} %pad_add_fusion.meta_ref, bf16[8,128,256]{2,1,0:T(8,128)(2,1)} %bitcast.27, bf16[2,128,256]{2,1,0:T(8,128)(2,1)} %bitcast.28, bf16[256,256]{1,0:T(8,128)(2,1)} %context_ref.1, bf16[16,128]{1,0:T(8,128)(2,1)} %fusion.4.ids_ref, ...), custom_call_target="tpu_custom_call" | custom-call | flops 10000000000 | bytes 20000000 | tf_op jit(solution)/shard_map/pallas_call | solution.py:486
  151.6 48.8 %shard_map.113 = (f32[1024,256]{1,0:T(8,128)}, f32[256,256]{1,0:T(8,128)}, f32[256,256]{1,0:T(8,128)}) custom-call(f32[1024,256]{1,0:T(8,128)} %get-tuple-element.6.a_ref, f32[256,256]{1,0:T(8,128)} %get-tuple-element.7.b_ref, f32[256,256]{1,0:T(8,128)} %get-tuple-element.8.c_ref), custom_call_target="tpu_custom_call" | custom-call | tf_op jit(solution)/shard_map/pallas_call | solution.py:544
  (11 shorter events, 0.1 us)

commit v4 on v3

--- a/solution.py
+++ b/solution.py
@@ -428,15 +428,10 @@
         lax.fori_loop(0, NB, drain, 0)
 
 
-def hand_over(a_ref, b_ref, c_ref, a_out, b_out, c_out, sem):
-    copies = [
-        pltpu.make_async_copy(src, dst, sem.at[k])
-        for k, (src, dst) in enumerate(((a_ref, a_out), (b_ref, b_out), (c_ref, c_out)))
-    ]
-    for cp in copies:
-        cp.start()
-    for cp in copies:
-        cp.wait()
+def hand_over(a_ref, b_ref, c_ref, a_out, b_out, c_out):
+    a_out[...] = a_ref[...]
+    b_out[...] = b_ref[...]
+    c_out[...] = c_ref[...]
 
 
 def local(
@@ -540,13 +535,11 @@
         ids16,
         tile_mask,
     )
-    anywhere = pl.BlockSpec(memory_space=pl.ANY)
     return pl.pallas_call(
         hand_over,
         out_shape=tuple(jax.ShapeDtypeStruct(a.shape, a.dtype) for a in (ugrad, igrad, cgrad)),
-        in_specs=[anywhere] * 3,
-        out_specs=(anywhere,) * 3,
-        scratch_shapes=[pltpu.SemaphoreType.DMA((3,))],
+        in_specs=[vmem] * 3,
+        out_specs=(vmem,) * 3,
     )(ugrad, igrad, cgrad)
 
 

time: 201 us -> 155 us (0.77)
  Pallas kernels: 196 us -> 149 us
    pallas_call x1, Pallas kernels: 48.8 us -> 2.5 us  [local(): pl.pallas_call(hand_over, out_shape=tuple((jax.ShapeDtypeStruct(a.shape,...]
where the time goes in v4:
time: 155 us; the launch traced here: 154 us
  Pallas kernels  149 us (96%)
  other arithmetic  2.68 us (2%)
    pallas_call x1, Pallas kernels, local(): pl.pallas_call(kernel, out_shape=(jax.ShapeDtypeStruct((1024, WIDTH), F32...  147 us

profile of v4, /device:TPU:0, one launch (start us, length us, event | category | flops | bytes accessed | tf_op | source)
XLA Modules:
  0.0 154.1 jit_solution(2173836099223084740)
XLA Ops:
  1.3 0.8 select_reduce_fusion
  2.1 0.1 fusion.1
  2.3 0.2 convert_reduce_fusion
  2.4 0.7 stack.21
  3.1 0.2 multiply_reduce_fusion
  3.3 0.1 convert_bitcast_fusion
  3.4 0.1 stack_tile.4
  3.5 0.1 compare_convert_fusion
  3.6 0.6 pad_add_fusion.meta_ref
  4.2 0.6 fusion.4.ids_ref
  4.8 146.8 %shard_map.112 = (f32[1024,256]{1,0:T(8,128)}, f32[256,256]{1,0:T(8,128)}, f32[256,256]{1,0:T(8,128)}) custom-call(s32[8,128]{1,0:T(8,128)} %pad_add_fusion.meta_ref, bf16[8,128,256]{2,1,0:T(8,128)(2,1)} %bitcast.27, bf16[2,128,256]{2,1,0:T(8,128)(2,1)} %bitcast.28, bf16[256,256]{1,0:T(8,128)(2,1)} %context_ref.1, bf16[16,128]{1,0:T(8,128)(2,1)} %fusion.4.ids_ref, ...), custom_call_target="tpu_custom_call" | custom-call | flops 10000000000 | bytes 20000000 | tf_op jit(solution)/shard_map/pallas_call | solution.py:481
  151.6 2.5 %shard_map.113 = (f32[1024,256]{1,0:T(8,128)}, f32[256,256]{1,0:T(8,128)}, f32[256,256]{1,0:T(8,128)}) custom-call(f32[1024,256]{1,0:T(8,128)} %get-tuple-element.6.a_ref, f32[256,256]{1,0:T(8,128)} %get-tuple-element.7.b_ref, f32[256,256]{1,0:T(8,128)} %get-tuple-element.8.c_ref), custom_call_target="tpu_custom_call" | custom-call | tf_op jit(solution)/shard_map/pallas_call | solution.py:538
  (11 shorter events, 0.1 us)

commit v5 on v4

--- a/solution.py
+++ b/solution.py
@@ -355,6 +355,7 @@
         cp.start()
         rcs.append(cp)
 
+    tick(1, 0)
     order = (1, 3, 2, 0)
     for d in order:
         theirs = lax.rem(s + d, 4)
@@ -366,8 +367,6 @@
         lax.fori_loop(0, 8, give, 0)
         piece = pl.ds(theirs * 8, 8)
         rstart(d, xs.at[piece], xr.at[piece], sib)
-        if d == 1:
-            tick(1, 0)
 
     def chip_sum(si, fi, h):
         return own_sum(blk(c, si, fi) + h).astype(F32) + xr[lax.rem(fi, 4) * 8 + lax.rem(si, 4) * 2 + h].astype(F32)
@@ -379,13 +378,16 @@
             for h in range(2):
                 r1s[d, e, h] = chip_sum(s + e, fi, h).astype(BF16)
             rstart(4 + 4 * d + e, r1s.at[d, e], r1r.at[d, e], speer[e])
-    tick(1, 1)
+        if d == 1:
+            tick(1, 1)
     tick(0, 3)
     cgrad_ref[...] = jnp.zeros_like(cgrad_ref)
 
     def ctx_dot(n, _):
         cgrad_ref[...] += jnp.dot(chot_a[n], call_a[n], preferred_element_type=F32)
         return 0
+
+    lax.fori_loop(0, 32, ctx_dot, 0)
 
     def plane_sum(d, h):
         total = chip_sum(s, f + d, h)
@@ -403,9 +405,8 @@
                 igrad_ref[pl.ds(h * SIDE, SIDE), :] = plane_sum(d, h)
         if d:
             rstart(20 + d, r2s.at[d], r2r.at[d], fpeer[d])
-        if d == 1:
+        if d == 2:
             tick(1, 2)
-            lax.fori_loop(0, 32, ctx_dot, 0)
     tick(1, 3)
     for n in range(8):
         rows = call_b[pl.ds(4 * n, 4)].reshape(SIDE, WIDTH)

time: 155 us -> 146 us (0.942)
  Pallas kernels: 149 us -> 140 us
    pallas_call x1, Pallas kernels: 147 us -> 138 us  [local(): pl.pallas_call(kernel, out_shape=(jax.ShapeDtypeStruct((1024, WIDTH), F32...]
where the time goes in v5:
time: 146 us; the launch traced here: 145 us
  Pallas kernels  140 us (96%)
  other arithmetic  2.68 us (2%)
    pallas_call x1, Pallas kernels, local(): pl.pallas_call(kernel, out_shape=(jax.ShapeDtypeStruct((1024, WIDTH), F32...  138 us

profile of v5, /device:TPU:0, one launch (start us, length us, event | category | flops | bytes accessed | tf_op | source)
XLA Modules:
  0.0 144.9 jit_solution(15558064034328627292)
XLA Ops:
  1.3 0.8 select_reduce_fusion
  2.1 0.1 fusion.1
  2.3 0.2 convert_reduce_fusion
  2.4 0.7 stack.21
  3.1 0.2 multiply_reduce_fusion
  3.3 0.1 convert_bitcast_fusion
  3.4 0.1 stack_tile.4
  3.5 0.1 compare_convert_fusion
  3.6 0.6 pad_add_fusion.meta_ref
  4.2 0.6 fusion.4.ids_ref
  4.8 137.6 %shard_map.112 = (f32[1024,256]{1,0:T(8,128)}, f32[256,256]{1,0:T(8,128)}, f32[256,256]{1,0:T(8,128)}) custom-call(s32[8,128]{1,0:T(8,128)} %pad_add_fusion.meta_ref, bf16[8,128,256]{2,1,0:T(8,128)(2,1)} %bitcast.27, bf16[2,128,256]{2,1,0:T(8,128)(2,1)} %bitcast.28, bf16[256,256]{1,0:T(8,128)(2,1)} %context_ref.1, bf16[16,128]{1,0:T(8,128)(2,1)} %fusion.4.ids_ref, ...), custom_call_target="tpu_custom_call" | custom-call | flops 10000000000 | bytes 20000000 | tf_op jit(solution)/shard_map/pallas_call | solution.py:482
  142.4 2.5 %shard_map.113 = (f32[1024,256]{1,0:T(8,128)}, f32[256,256]{1,0:T(8,128)}, f32[256,256]{1,0:T(8,128)}) custom-call(f32[1024,256]{1,0:T(8,128)} %get-tuple-element.6.a_ref, f32[256,256]{1,0:T(8,128)} %get-tuple-element.7.b_ref, f32[256,256]{1,0:T(8,128)} %get-tuple-element.8.c_ref), custom_call_target="tpu_custom_call" | custom-call | tf_op jit(solution)/shard_map/pallas_call | solution.py:539
  (11 shorter events, 0.1 us)

commit v6 on v5

--- a/solution.py
+++ b/solution.py
@@ -21,11 +21,17 @@
 
 def kernel(
     meta_ref,
+    users_in,
+    shard_in,
+    context_in,
+    ids_in,
+    mask_in,
+    ugrad_out,
+    igrad_out,
+    cgrad_out,
     users_ref,
-    shard_ref,
     context_ref,
     ids_ref,
-    mask_hbm,
     ugrad_ref,
     igrad_ref,
     cgrad_ref,
@@ -54,7 +60,8 @@
     r1r,
     r2s,
     r2r,
-    mask_sem,
+    in_sem,
+    out_sem,
     ag_send,
     ag_recv,
     z_send,
@@ -86,8 +93,21 @@
     fpeer = {d: dev(f + d, s) for d in turns}
     speer = {d: dev(f, s + d) for d in turns}
     partners = tuple(fpeer.values()) + tuple(speer.values()) + (devz(1), devz(-1), sib)
-    mask_copy = pltpu.make_async_copy(mask_hbm, mask, mask_sem)
-    mask_copy.start()
+    mine = ((c * 4 + s) * 4 + f) * 2
+    fetch = [
+        pltpu.make_async_copy(src, dst, in_sem.at[k])
+        for k, (src, dst) in enumerate(
+            (
+                (shard_in, items.at[pl.ds(mine, 2)]),
+                (context_in, context_ref),
+                (ids_in, ids_ref),
+                (users_in, users_ref),
+                (mask_in, mask),
+            )
+        )
+    ]
+    for cp in fetch:
+        cp.start()
     barrier = pltpu.get_barrier_semaphore()
     for p in partners:
         pl.semaphore_signal(barrier, inc=1, device_id=p, device_id_type=MESH)
@@ -103,9 +123,9 @@
     def blk(ci, si, fi):
         return ((ci * 4 + lax.rem(si + 4, 4)) * 4 + lax.rem(fi + 4, 4)) * 2
 
-    def ag(k, start, size, to, src=None):
+    def ag(k, start, size, to):
         view = items.at[pl.ds(start, size)]
-        cp = rcopy(view if src is None else src, view, ag_send.at[k], ag_recv.at[k], to)
+        cp = rcopy(view, view, ag_send.at[k], ag_recv.at[k], to)
         cp.start()
         started.append(cp)
 
@@ -113,12 +133,12 @@
         view = items.at[pl.ds(start, size)]
         rcopy(view, view, ag_send.at[k], ag_recv.at[k], sib).wait_recv()
 
-    mine = blk(c, s, f)
+    fetch[0].wait()
     for d in turns:
-        ag(d, mine, 2, fpeer[d], shard_ref)
+        ag(d, mine, 2, fpeer[d])
     for d in turns:
-        ag(4 + d, mine, 2, speer[d], shard_ref)
-    items[pl.ds(mine, 2)] = shard_ref[...]
+        ag(4 + d, mine, 2, speer[d])
+    fetch[1].wait()
     ctx32[...] = context_ref[...].astype(F32)
     ugrad_ref[...] = jnp.zeros_like(ugrad_ref)
     run[...] = jnp.zeros_like(run)
@@ -129,13 +149,20 @@
         for dd in turns:
             ag(4 + 4 * e + dd, blk(c, s, f + e), 2, speer[dd])
     ag(20, blk(c, s, 0 * f), 8, sib)
+    last = tuple(zip((0, 3, 1, 2), (22, 24, 25, 26)))
     for d in turns:
-        for e in (0, 3, 1, 2):
+        for e, k in last:
             got(4 + 4 * e + d, blk(c, s - d, f + e), 2)
-        ag(20 + d, blk(c, s - d, 0 * f), 8, sib)
-    for d in (0, 1, 3, 2):
+            if d == 2:
+                ag(k, blk(c, s - d, f + e), 2, sib)
+        if d != 2:
+            ag(20 + d, blk(c, s - d, 0 * f), 8, sib)
+    for d in (0, 1, 3):
         got(20 + d, blk(1 - c, f - d, 0 * f), 8)
-    mask_copy.wait()
+    for e, k in last:
+        got(k, blk(1 - c, f - 2, s + e), 2)
+    for cp in fetch[2:]:
+        cp.wait()
 
     right, left = devz(1), devz(-1)
 
@@ -184,19 +211,22 @@
     def predict(j):
         slot = lax.rem(j, 4)
 
+        far = lax.rem(z + 2, 4)
+
         def tile(n, _):
-            o, k = n // PER, lax.rem(n, PER)
-            p = j * 16 + n
+            o, k = lax.rem(far + n // PER, 4), lax.rem(n, PER)
+            p = j * 16 + o * PER + k
             pr = lax.dot_general(
                 users_ref[meta_ref[USER, p]], item_context(p), (((1,), (1,)), ((), ())), preferred_element_type=F32
             )
             part[slot, o, k] = pr
             return 0
 
-        lax.fori_loop(0, 16, tile, 0)
-        send1[j] = part[slot, lax.rem(z + 2, 4)].astype(BF16)
+        lax.fori_loop(0, PER, tile, 0)
+        send1[j] = part[slot, far].astype(BF16)
         for cp in zcopies(0, j):
             cp.start()
+        lax.fori_loop(PER, 16, tile, 0)
 
     def combine(j):
         slot = lax.rem(j, 4)
@@ -225,28 +255,42 @@
         for cp in zcopies(3, j):
             cp.start()
 
+    def user_part(j, o):
+        for k in range(PER):
+            p = j * 16 + o * PER + k
+            r = resid[j, o, k]
+            u = meta_ref[USER, p]
+            for b in range(8):
+                ahot[pl.ds(b * SIDE, SIDE), pl.ds(k * SIDE, SIDE)] = jnp.where(u == b, r, jnp.zeros_like(r))
+            icb[pl.ds(k * SIDE, SIDE), :] = item_context(p)
+        ugrad_ref[...] += jnp.dot(ahot[...], icb[...], preferred_element_type=F32)
+
+    def item_part(j, o):
+        for k in range(PER):
+            p = j * 16 + o * PER + k
+            it = items[meta_ref[PLACE, p]].astype(F32)
+            cr = ctx32[pl.ds(meta_ref[CTXT, p], 1), :]
+            q = lax.dot_general(
+                resid[j, o, k], users_ref[meta_ref[USER, p]], (((0,), (0,)), ((), ())), preferred_element_type=F32
+            )
+            cterm[pl.ds(p, 1), :] = jnp.sum(it * q, axis=0, keepdims=True)
+            total = run[...] * meta_ref[KEEP, p].astype(F32) + q * cr
+            run[...] = total
+            segs[p] = total.astype(BF16)
+
     def gradients(j):
+        def near(n, _):
+            user_part(j, lax.rem(z + 3 + n, 4))
+            return 0
+
+        def group(o, _):
+            item_part(j, o)
+            return 0
+
+        lax.fori_loop(0, 3, near, 0)
         zwait(3, j)
-
-        def group(o, _):
-            for k in range(PER):
-                p = j * 16 + o * PER + k
-                r = resid[j, o, k]
-                u = meta_ref[USER, p]
-                for b in range(8):
-                    ahot[pl.ds(b * SIDE, SIDE), pl.ds(k * SIDE, SIDE)] = jnp.where(u == b, r, jnp.zeros_like(r))
-                it = items[meta_ref[PLACE, p]].astype(F32)
-                cr = ctx32[pl.ds(meta_ref[CTXT, p], 1), :]
-                icb[pl.ds(k * SIDE, SIDE), :] = (it * cr).astype(BF16)
-                q = lax.dot_general(r, users_ref[u], (((0,), (0,)), ((), ())), preferred_element_type=F32)
-                cterm[pl.ds(p, 1), :] = jnp.sum(it * q, axis=0, keepdims=True)
-                total = run[...] * meta_ref[KEEP, p].astype(F32) + q * cr
-                run[...] = total
-                segs[p] = total.astype(BF16)
-            ugrad_ref[...] += jnp.dot(ahot[...], icb[...], preferred_element_type=F32)
-            return 0
-
         lax.fori_loop(0, 4, group, 0)
+        user_part(j, lax.rem(z + 2, 4))
 
     def ccopies(g, k, arriving):
         pos = lambda si, fi: (c * 4 + lax.rem(si + 4, 4)) * 4 + lax.rem(fi + 4, 4)
@@ -356,8 +400,14 @@
         rcs.append(cp)
 
     tick(1, 0)
+    results = [
+        pltpu.make_async_copy(src, dst, out_sem.at[k])
+        for k, (src, dst) in enumerate(((ugrad_ref, ugrad_out), (igrad_ref, igrad_out), (cgrad_ref, cgrad_out)))
+    ]
+    results[0].start()
     order = (1, 3, 2, 0)
-    for d in order:
+
+    def give_piece(d):
         theirs = lax.rem(s + d, 4)
 
         def give(n, _):
@@ -367,6 +417,9 @@
         lax.fori_loop(0, 8, give, 0)
         piece = pl.ds(theirs * 8, 8)
         rstart(d, xs.at[piece], xr.at[piece], sib)
+
+    give_piece(1)
+    give_piece(3)
 
     def chip_sum(si, fi, h):
         return own_sum(blk(c, si, fi) + h).astype(F32) + xr[lax.rem(fi, 4) * 8 + lax.rem(si, 4) * 2 + h].astype(F32)
@@ -379,7 +432,10 @@
                 r1s[d, e, h] = chip_sum(s + e, fi, h).astype(BF16)
             rstart(4 + 4 * d + e, r1s.at[d, e], r1r.at[d, e], speer[e])
         if d == 1:
+            give_piece(2)
             tick(1, 1)
+        if d == 3:
+            give_piece(0)
     tick(0, 3)
     cgrad_ref[...] = jnp.zeros_like(cgrad_ref)
 
@@ -415,6 +471,8 @@
         rgot(20 + d, r2r.at[d])
         igrad_ref[...] += r2r[d].reshape(2 * SIDE, WIDTH).astype(F32)
 
+    results[1].start()
+    results[2].start()
     for cp in started + rcs:
         cp.wait_send()
     for g in range(3):
@@ -427,12 +485,21 @@
             return 0
 
         lax.fori_loop(0, NB, drain, 0)
-
-
-def hand_over(a_ref, b_ref, c_ref, a_out, b_out, c_out):
-    a_out[...] = a_ref[...]
-    b_out[...] = b_ref[...]
-    c_out[...] = c_ref[...]
+    for cp in results:
+        cp.wait()
+
+
+def hand_over(*refs):
+    srcs, dsts, bufs, sem = refs[:3], refs[3:6], refs[6:9], refs[9]
+    reads = [pltpu.make_async_copy(a, b, sem.at[0, k]) for k, (a, b) in enumerate(zip(srcs, bufs))]
+    writes = [pltpu.make_async_copy(a, b, sem.at[1, k]) for k, (a, b) in enumerate(zip(bufs, dsts))]
+    for cp in reads:
+        cp.start()
+    for a, b in zip(reads, writes):
+        a.wait()
+        b.start()
+    for cp in writes:
+        cp.wait()
 
 
 def local(
@@ -476,7 +543,7 @@
     rows = jnp.stack([ctx_s, jnp.tile(ctx_s[ROWS_A:], n // ROWS_B)])
     ids16 = jnp.pad(rows, ((0, 14), (0, 0))).astype(BF16)
     smem = pl.BlockSpec(memory_space=pltpu.SMEM)
-    vmem = pl.BlockSpec(memory_space=pltpu.VMEM)
+    anywhere = pl.BlockSpec(memory_space=pl.ANY)
     tile2 = (SIDE, SIDE)
     wide = (SIDE, WIDTH)
     ugrad, igrad, cgrad = pl.pallas_call(
@@ -486,9 +553,15 @@
             jax.ShapeDtypeStruct((2 * SIDE, WIDTH), F32),
             jax.ShapeDtypeStruct((nctx, WIDTH), F32),
         ),
-        in_specs=[smem] + [vmem] * 4 + [pl.BlockSpec(memory_space=pl.ANY)],
-        out_specs=(vmem,) * 3,
+        in_specs=[smem] + [anywhere] * 5,
+        out_specs=(anywhere,) * 3,
         scratch_shapes=[
+            pltpu.VMEM((8,) + wide, BF16),
+            pltpu.VMEM((nctx, WIDTH), BF16),
+            pltpu.VMEM((16, SIDE), BF16),
+            pltpu.VMEM((1024, WIDTH), F32),
+            pltpu.VMEM((2 * SIDE, WIDTH), F32),
+            pltpu.VMEM((nctx, WIDTH), F32),
             pltpu.VMEM((64,) + wide, BF16),
             pltpu.VMEM((n,) + tile2, jnp.int32),
             pltpu.VMEM((nctx, WIDTH), F32),
@@ -514,9 +587,10 @@
             pltpu.VMEM((4, 4, 2) + wide, BF16),
             pltpu.VMEM((4, 2) + wide, BF16),
             pltpu.VMEM((4, 2) + wide, BF16),
-            pltpu.SemaphoreType.DMA,
-            pltpu.SemaphoreType.DMA((24,)),
-            pltpu.SemaphoreType.DMA((24,)),
+            pltpu.SemaphoreType.DMA((5,)),
+            pltpu.SemaphoreType.DMA((3,)),
+            pltpu.SemaphoreType.DMA((27,)),
+            pltpu.SemaphoreType.DMA((27,)),
             pltpu.SemaphoreType.DMA((4, NB, 2)),
             pltpu.SemaphoreType.DMA((4, NB, 2)),
             pltpu.SemaphoreType.DMA((3, 9)),
@@ -539,8 +613,10 @@
     return pl.pallas_call(
         hand_over,
         out_shape=tuple(jax.ShapeDtypeStruct(a.shape, a.dtype) for a in (ugrad, igrad, cgrad)),
-        in_specs=[vmem] * 3,
-        out_specs=(vmem,) * 3,
+        in_specs=[anywhere] * 3,
+        out_specs=(anywhere,) * 3,
+        scratch_shapes=[pltpu.VMEM(a.shape, a.dtype) for a in (ugrad, igrad, cgrad)]
+        + [pltpu.SemaphoreType.DMA((2, 3))],
     )(ugrad, igrad, cgrad)
 
 

time: 146 us -> 143 us (0.979)
  Pallas kernels: 140 us -> 138 us
    pallas_call x1, Pallas kernels: 138 us -> 135 us  [local(): pl.pallas_call(kernel, out_shape=(jax.ShapeDtypeStruct((1024, WIDTH), F32...]
where the time goes in v6:
time: 143 us; the launch traced here: 142 us
  Pallas kernels  138 us (97%)
  other arithmetic  2.68 us (2%)
    pallas_call x1, Pallas kernels, local(): pl.pallas_call(kernel, out_shape=(jax.ShapeDtypeStruct((1024, WIDTH), F32...  135 us

profile of v6, /device:TPU:0, one launch (start us, length us, event | category | flops | bytes accessed | tf_op | source)
XLA Modules:
  0.0 142.4 jit_solution(12287264108332118892)
XLA Ops:
  1.3 0.8 select_reduce_fusion
  2.1 0.1 fusion.1
  2.3 0.2 convert_reduce_fusion
  2.4 0.7 stack.21
  3.1 0.2 multiply_reduce_fusion
  3.3 0.1 convert_bitcast_fusion
  3.4 0.1 stack_tile.4
  3.5 0.1 compare_convert_fusion
  3.6 0.6 pad_add_fusion.meta_ref
  4.2 0.6 fusion.4.ids_in
  4.8 135.1 %shard_map.112 = (f32[1024,256]{1,0:T(8,128)}, f32[256,256]{1,0:T(8,128)}, f32[256,256]{1,0:T(8,128)}) custom-call(s32[8,128]{1,0:T(8,128)} %pad_add_fusion.meta_ref, bf16[8,128,256]{2,1,0:T(8,128)(2,1)} %bitcast.27, bf16[2,128,256]{2,1,0:T(8,128)(2,1)} %bitcast.28, bf16[256,256]{1,0:T(8,128)(2,1)} %context_in.1, bf16[16,128]{1,0:T(8,128)(2,1)} %fusion.4.ids_in, ...), custom_call_target="tpu_custom_call" | custom-call | flops 10000000000 | bytes 20000000 | tf_op jit(solution)/shard_map/pallas_call | solution.py:549
  140.0 2.4 %shard_map.113 = (f32[1024,256]{1,0:T(8,128)}, f32[256,256]{1,0:T(8,128)}, f32[256,256]{1,0:T(8,128)}) custom-call(f32[1024,256]{1,0:T(8,128)} %get-tuple-element.6.refs_0_, f32[256,256]{1,0:T(8,128)} %get-tuple-element.7.refs_1_, f32[256,256]{1,0:T(8,128)} %get-tuple-element.8.refs_2_), custom_call_target="tpu_custom_call" | custom-call | tf_op jit(solution)/shard_map/pallas_call | solution.py:613
  (11 shorter events, 0.1 us)

commit v7 on v6

--- a/solution.py
+++ b/solution.py
@@ -444,6 +444,19 @@
         return 0
 
     lax.fori_loop(0, 32, ctx_dot, 0)
+    for cp in started:
+        cp.wait_send()
+    for ph in range(4):
+        def drain(j, _):
+            for cp in zcopies(ph, j):
+                cp.wait_send()
+            return 0
+
+        lax.fori_loop(0, NB, drain, 0)
+    legs = (1, 2, 3, 5, 6, 7, 8)
+    for g in (0, 2):
+        for k in legs:
+            ccopies(g, k, False).wait_send()
 
     def plane_sum(d, h):
         total = chip_sum(s, f + d, h)
@@ -473,18 +486,10 @@
 
     results[1].start()
     results[2].start()
-    for cp in started + rcs:
+    for cp in rcs:
         cp.wait_send()
-    for g in range(3):
-        for k in (1, 2, 3, 5, 6, 7, 8):
-            ccopies(g, k, False).wait_send()
-    for ph in range(4):
-        def drain(j, _):
-            for cp in zcopies(ph, j):
-                cp.wait_send()
-            return 0
-
-        lax.fori_loop(0, NB, drain, 0)
+    for k in legs:
+        ccopies(1, k, False).wait_send()
     for cp in results:
         cp.wait()
 

time: 143 us -> 143 us (level)
  no operation moved by 1% of the time
where the time goes in v7:
time: 143 us; the launch traced here: 142 us
  Pallas kernels  137 us (96%)
  other arithmetic  2.68 us (2%)
    pallas_call x1, Pallas kernels, local(): pl.pallas_call(kernel, out_shape=(jax.ShapeDtypeStruct((1024, WIDTH), F32...  135 us

profile of v7, /device:TPU:0, one launch (start us, length us, event | category | flops | bytes accessed | tf_op | source)
XLA Modules:
  0.0 142.0 jit_solution(514296062388036972)
XLA Ops:
  1.3 0.8 select_reduce_fusion
  2.1 0.1 fusion.1
  2.3 0.2 convert_reduce_fusion
  2.4 0.7 stack.21
  3.1 0.2 multiply_reduce_fusion
  3.3 0.1 convert_bitcast_fusion
  3.4 0.1 stack_tile.4
  3.5 0.1 compare_convert_fusion
  3.6 0.6 pad_add_fusion.meta_ref
  4.2 0.6 fusion.4.ids_in
  4.8 134.8 %shard_map.112 = (f32[1024,256]{1,0:T(8,128)}, f32[256,256]{1,0:T(8,128)}, f32[256,256]{1,0:T(8,128)}) custom-call(s32[8,128]{1,0:T(8,128)} %pad_add_fusion.meta_ref, bf16[8,128,256]{2,1,0:T(8,128)(2,1)} %bitcast.27, bf16[2,128,256]{2,1,0:T(8,128)(2,1)} %bitcast.28, bf16[256,256]{1,0:T(8,128)(2,1)} %context_in.1, bf16[16,128]{1,0:T(8,128)(2,1)} %fusion.4.ids_in, ...), custom_call_target="tpu_custom_call" | custom-call | flops 10000000000 | bytes 20000000 | tf_op jit(solution)/shard_map/pallas_call | solution.py:554
  139.6 2.4 %shard_map.113 = (f32[1024,256]{1,0:T(8,128)}, f32[256,256]{1,0:T(8,128)}, f32[256,256]{1,0:T(8,128)}) custom-call(f32[1024,256]{1,0:T(8,128)} %get-tuple-element.6.refs_0_, f32[256,256]{1,0:T(8,128)} %get-tuple-element.7.refs_1_, f32[256,256]{1,0:T(8,128)} %get-tuple-element.8.refs_2_), custom_call_target="tpu_custom_call" | custom-call | tf_op jit(solution)/shard_map/pallas_call | solution.py:618
  (11 shorter events, 0.1 us)

commit v8 on v7

--- a/solution.py
+++ b/solution.py
@@ -136,23 +136,38 @@
     fetch[0].wait()
     for d in turns:
         ag(d, mine, 2, fpeer[d])
-    for d in turns:
+    for d in (1, 3):
         ag(4 + d, mine, 2, speer[d])
     fetch[1].wait()
     ctx32[...] = context_ref[...].astype(F32)
     ugrad_ref[...] = jnp.zeros_like(ugrad_ref)
     run[...] = jnp.zeros_like(run)
     call_a[...] = jnp.zeros_like(call_a)
+
+    def relay(e):
+        for d in (1, 3):
+            h = d // 2
+            got(4 + 4 * e + d, blk(c, s - d, f + e), 2)
+            ag((4 + 4 * e + 2, 27 + e)[h], blk(c, s - d, f + e) + h, 1, speer[d])
+
     for d in turns:
         e = 4 - d
         got(d, blk(c, s, f + e), 2)
-        for dd in turns:
+        for dd in turns if e == 2 else (1, 3):
             ag(4 + 4 * e + dd, blk(c, s, f + e), 2, speer[dd])
+        if e != 2:
+            relay(0 if e == 3 else 3)
     ag(20, blk(c, s, 0 * f), 8, sib)
     last = tuple(zip((0, 3, 1, 2), (22, 24, 25, 26)))
     for d in turns:
+        if d == 1:
+            relay(1)
         for e, k in last:
-            got(4 + 4 * e + d, blk(c, s - d, f + e), 2)
+            if e == 2:
+                got(4 + 4 * e + d, blk(c, s - d, f + e), 2)
+            elif d == 2:
+                got(4 + 4 * e + 2, blk(c, s - 2, f + e), 1)
+                got(27 + e, blk(c, s - 2, f + e) + 1, 1)
             if d == 2:
                 ag(k, blk(c, s - d, f + e), 2, sib)
         if d != 2:
@@ -594,8 +609,8 @@
             pltpu.VMEM((4, 2) + wide, BF16),
             pltpu.SemaphoreType.DMA((5,)),
             pltpu.SemaphoreType.DMA((3,)),
-            pltpu.SemaphoreType.DMA((27,)),
-            pltpu.SemaphoreType.DMA((27,)),
+            pltpu.SemaphoreType.DMA((31,)),
+            pltpu.SemaphoreType.DMA((31,)),
             pltpu.SemaphoreType.DMA((4, NB, 2)),
             pltpu.SemaphoreType.DMA((4, NB, 2)),
             pltpu.SemaphoreType.DMA((3, 9)),

time: 143 us -> 140 us (0.979)
  Pallas kernels: 137 us -> 135 us
    pallas_call x1, Pallas kernels: 135 us -> 133 us  [local(): pl.pallas_call(kernel, out_shape=(jax.ShapeDtypeStruct((1024, WIDTH), F32...]
where the time goes in v8:
time: 140 us
  Pallas kernels  135 us (96%)
  other arithmetic  2.68 us (2%)
    pallas_call x1, Pallas kernels, local(): pl.pallas_call(kernel, out_shape=(jax.ShapeDtypeStruct((1024, WIDTH), F32...  133 us

profile of v8, /device:TPU:0, one launch (start us, length us, event | category | flops | bytes accessed | tf_op | source)
XLA Modules:
  0.0 139.8 jit_solution(13512034174058475424)
XLA Ops:
  1.3 0.8 select_reduce_fusion
  2.1 0.1 fusion.1
  2.3 0.2 convert_reduce_fusion
  2.4 0.7 stack.21
  3.1 0.2 multiply_reduce_fusion
  3.3 0.1 convert_bitcast_fusion
  3.4 0.1 stack_tile.4
  3.5 0.1 compare_convert_fusion
  3.6 0.6 pad_add_fusion.meta_ref
  4.2 0.6 fusion.4.ids_in
  4.8 132.6 %shard_map.112 = (f32[1024,256]{1,0:T(8,128)}, f32[256,256]{1,0:T(8,128)}, f32[256,256]{1,0:T(8,128)}) custom-call(s32[8,128]{1,0:T(8,128)} %pad_add_fusion.meta_ref, bf16[8,128,256]{2,1,0:T(8,128)(2,1)} %bitcast.27, bf16[2,128,256]{2,1,0:T(8,128)(2,1)} %bitcast.28, bf16[256,256]{1,0:T(8,128)(2,1)} %context_in.1, bf16[16,128]{1,0:T(8,128)(2,1)} %fusion.4.ids_in, ...), custom_call_target="tpu_custom_call" | custom-call | flops 10000000000 | bytes 20000000 | tf_op jit(solution)/shard_map/pallas_call | solution.py:569
  137.4 2.4 %shard_map.113 = (f32[1024,256]{1,0:T(8,128)}, f32[256,256]{1,0:T(8,128)}, f32[256,256]{1,0:T(8,128)}) custom-call(f32[1024,256]{1,0:T(8,128)} %get-tuple-element.6.refs_0_, f32[256,256]{1,0:T(8,128)} %get-tuple-element.7.refs_1_, f32[256,256]{1,0:T(8,128)} %get-tuple-element.8.refs_2_), custom_call_target="tpu_custom_call" | custom-call | tf_op jit(solution)/shard_map/pallas_call | solution.py:633
  (11 shorter events, 0.1 us)
